TPU v7x, 32 devices: a whole 2x2x4 slice. The times are simulated.
32 devices in a mesh: batch: 8 (over y, x, core), head: 4 (over z).
Axes of the slice: x: 2, y: 2, z: 4, core: 2. Of those that a mesh axis runs over, the one named last changes fastest.
Arguments:
- tokens: bfloat16 [24576, 768], P(('batch', 'head')), may hold values from -6 to 6
- query_weight: bfloat16 [768, 768], P(None, 'head'), may hold values from -0.21875 to 0.21875
- key_weight: bfloat16 [768, 768], P(None, 'head'), may hold values from -0.21875 to 0.21875
- value_weight: bfloat16 [768, 768], P(None, 'head'), may hold values from -0.21875 to 0.21875
- query_bias: float32 [768], P('head'), may hold values from -3 to 3
- value_bias: float32 [768], P('head'), may hold values from -3 to 3
- mixer_weight: bfloat16 [768, 768], replicated, may hold values from -1.25 to 1.25
- mixer_bias: float32 [768], replicated, may hold values from -2 to 2
- first_gain: float32 [768], replicated, may hold values from 0.5 to 1.5
- first_shift: float32 [768], replicated, may hold values from -2 to 2
- expand_weight: bfloat16 [768, 3072], replicated, may hold values from -0.21875 to 0.21875
- expand_bias: float32 [3072], replicated, may hold values from -3 to 3
- reduce_weight: bfloat16 [3072, 768], replicated, may hold values from -0.109375 to 0.109375
- reduce_bias: float32 [768], replicated, may hold values from -2 to 2
- second_gain: float32 [768], replicated, may hold values from 0.5 to 1.5
- second_shift: float32 [768], replicated, may hold values from -2 to 2
- cotangent: bfloat16 [24576, 768], P(('batch', 'head')), may hold values from -6 to 6
- group_kinds: int32 [8], P('batch'), may hold values from 0 to 1
- pair_orders: int32 [24, 12, 2], P('batch', 'head'), may hold values from 0 to 1, each once within a row
- triple_orders: int32 [16, 12, 3], P('batch', 'head'), may hold values from 0 to 2, each once within a row
Outputs:
- layer_output: bfloat16 [24576, 768], P(('batch', 'head'))
- tokens_grad: bfloat16 [24576, 768], P(('batch', 'head'))
- query_weight_grad: float32 [768, 768], P(None, 'head')
- key_weight_grad: float32 [768, 768], P(None, 'head')
- value_weight_grad: float32 [768, 768], P(None, 'head')
- query_bias_grad: float32 [768], P('head')
- value_bias_grad: float32 [768], P('head')
- mixer_weight_grad: float32 [768, 768], P('head')
- mixer_bias_grad: float32 [768], replicated
- first_gain_grad: float32 [768], replicated
- first_shift_grad: float32 [768], replicated
- expand_weight_grad: float32 [768, 3072], P(None, 'head')
- expand_bias_grad: float32 [3072], replicated
- reduce_weight_grad: float32 [3072, 768], P('head')
- reduce_bias_grad: float32 [768], replicated
- second_gain_grad: float32 [768], replicated
- second_shift_grad: float32 [768], replicated
Inputs may be any that keep to these rules, and one draw needn't show every extreme that they name: `group_kinds`: 0: the group's six blocks are three sequences of two blocks; 1: two sequences of three blocks. Each pair_orders[s, h, :] is a permutation. Each triple_orders[s, h, :] is a permutation.
All inputs are finite; a program needn't handle non-finite values.
Results may differ from a plain program's by a relative error of at most 0.018.
Values may be sent and summed in bfloat16 or wider, within the bound.
A program may use at most 192 MiB of HBM per device.

v0:
```python
import math

import jax
import jax.numpy as jnp
from jax import lax
from jax.sharding import PartitionSpec as P

HEAD_SIZE = 64
BLOCK = 512


EPSILON = 1e-05


def product(matrix_a, matrix_b):
    return jnp.dot(matrix_a, matrix_b, preferred_element_type=jnp.float32)


def product_tn(matrix_a, matrix_b):
    return lax.dot_general(
        matrix_a, matrix_b, (((0,), (0,)), ((), ())), preferred_element_type=jnp.float32
    )


def product_nt(matrix_a, matrix_b):
    return lax.dot_general(
        matrix_a, matrix_b, (((1,), (1,)), ((), ())), preferred_element_type=jnp.float32
    )


def exact_gelu(values):
    return jax.nn.gelu(values, approximate=False)


def norm_forward(values, gain_vec, shift_vec):
    center = values - jnp.mean(values, axis=-1, keepdims=True)
    inverse = lax.rsqrt(jnp.mean(center * center, axis=-1, keepdims=True) + EPSILON)
    scaled = center * inverse
    return (scaled * gain_vec + shift_vec, scaled, inverse)


def norm_backward(upstream, gain_vec, scaled, inverse):
    inner_term = upstream * gain_vec
    inner_mean = jnp.mean(inner_term, axis=-1, keepdims=True)
    cross_mean = jnp.mean(inner_term * scaled, axis=-1, keepdims=True)
    delta = inverse * (inner_term - inner_mean - scaled * cross_mean)
    return (delta, jnp.sum(upstream * scaled, axis=0), jnp.sum(upstream, axis=0))


def key_blocks(group_kinds, pair_orders, triple_orders):
    block_count = group_kinds.shape[0] * 6
    block_ids = jnp.arange(block_count, dtype=jnp.int32)
    group_ids = block_ids // 6
    position = block_ids % 6
    first_block = group_ids * 6
    pair_pick = pair_orders[group_ids * 3 + position // 2, :, position % 2]
    triple_pick = triple_orders[group_ids * 2 + position // 3, :, position % 3]
    pair_key = (first_block + 2 * (position // 2))[:, None] + pair_pick
    triple_key = (first_block + 3 * (position // 3))[:, None] + triple_pick
    use_pairs = (group_kinds[group_ids] == 0)[:, None]
    return jnp.where(use_pairs, pair_key, triple_key)


def per_device(
    tokens,
    query_weight,
    key_weight,
    value_weight,
    query_bias,
    value_bias,
    mixer_weight,
    mixer_bias,
    first_gain,
    first_shift,
    expand_weight,
    expand_bias,
    reduce_weight,
    reduce_bias,
    second_gain,
    second_shift,
    cotangent,
    group_kinds,
    pair_orders,
    triple_orders,
):
    head_width = query_weight.shape[1]
    local_heads = head_width // HEAD_SIZE
    score_scale = 1.0 / math.sqrt(HEAD_SIZE)
    chosen = key_blocks(group_kinds, pair_orders, triple_orders)
    head_ids = jnp.arange(local_heads, dtype=jnp.int32)[None, :]
    gathered = lax.all_gather(tokens, "head", axis=0, tiled=True)
    all_rows = gathered.shape[0]
    block_shape = (all_rows // BLOCK, BLOCK, local_heads, HEAD_SIZE)
    queries = (product(gathered, query_weight) + query_bias).astype(jnp.bfloat16)
    keys = product(gathered, key_weight).astype(jnp.bfloat16)
    values_low = (product(gathered, value_weight) + value_bias).astype(jnp.bfloat16)
    query_quad = queries.reshape(block_shape)
    key_sel = keys.reshape(block_shape)[chosen, :, head_ids, :]
    value_sel = values_low.reshape(block_shape)[chosen, :, head_ids, :]

    def attend_block(operands):
        query_blk, key_blk, value_blk = operands
        scores = (
            jnp.einsum("qhe,hke->hqk", query_blk, key_blk, preferred_element_type=jnp.float32)
            * score_scale
        )
        row_max = jnp.max(scores, axis=-1, keepdims=True)
        raised = jnp.exp(scores - row_max)
        row_total = jnp.sum(raised, axis=-1, keepdims=True)
        weights = (raised / row_total).astype(jnp.bfloat16)
        result = jnp.einsum("hqk,hke->qhe", weights, value_blk, preferred_element_type=jnp.float32)
        return (result.astype(jnp.bfloat16), (row_max + jnp.log(row_total))[..., 0])

    attended, log_totals = lax.map(attend_block, (query_quad, key_sel, value_sel))
    attended_rows = attended.reshape(all_rows, head_width)
    token_values = tokens.astype(jnp.float32)
    mixed_in = lax.all_to_all(attended_rows, "head", split_axis=0, concat_axis=1, tiled=True)
    mixed = product(mixed_in, mixer_weight)
    mixed = mixed + mixer_bias + token_values
    normed, first_scaled, first_inverse = norm_forward(mixed, first_gain, first_shift)
    normed_low = normed.astype(jnp.bfloat16)
    hidden = product(normed_low, expand_weight) + expand_bias
    active, gelu_pullback = jax.vjp(exact_gelu, hidden)
    active_low = active.astype(jnp.bfloat16)
    branch_sum = product(active_low, reduce_weight) + reduce_bias + normed
    layer_output, second_scaled, second_inverse = norm_forward(
        branch_sum, second_gain, second_shift
    )
    upstream = cotangent.astype(jnp.float32)
    branch_delta, second_gain_grad, second_shift_grad = norm_backward(
        upstream, second_gain, second_scaled, second_inverse
    )
    reduce_delta = branch_delta.astype(jnp.bfloat16)
    reduce_bias_grad = jnp.sum(reduce_delta.astype(jnp.float32), axis=0)
    reduce_weight_grad = product_tn(active_low, reduce_delta)
    (hidden_pre,) = gelu_pullback(product_nt(reduce_delta, reduce_weight))
    hidden_delta = hidden_pre.astype(jnp.bfloat16)
    expand_bias_grad = jnp.sum(hidden_delta.astype(jnp.float32), axis=0)
    expand_weight_grad = product_tn(normed_low, hidden_delta)
    normed_delta = product_nt(hidden_delta, expand_weight) + branch_delta
    mixed_delta, first_gain_grad, first_shift_grad = norm_backward(
        normed_delta, first_gain, first_scaled, first_inverse
    )
    mixer_delta = mixed_delta.astype(jnp.bfloat16)
    mixer_bias_grad = jnp.sum(mixer_delta.astype(jnp.float32), axis=0)
    mixer_full = product_tn(mixed_in, mixer_delta)
    attended_back = product_nt(mixer_delta, mixer_weight).astype(jnp.bfloat16)
    attended_delta = lax.all_to_all(attended_back, "head", split_axis=1, concat_axis=0, tiled=True)
    expand_share, reduce_share, mixer_share = (
        lax.psum_scatter(
            expand_weight_grad.astype(jnp.bfloat16), "head", scatter_dimension=1, tiled=True
        ).astype(jnp.float32),
        lax.psum_scatter(
            reduce_weight_grad.astype(jnp.bfloat16), "head", scatter_dimension=0, tiled=True
        ).astype(jnp.float32),
        lax.psum_scatter(
            mixer_full.astype(jnp.bfloat16), "head", scatter_dimension=0, tiled=True
        ).astype(jnp.float32),
    )
    vector_total = lax.psum(
        (
            mixer_bias_grad,
            first_gain_grad,
            first_shift_grad,
            expand_bias_grad,
            reduce_bias_grad,
            second_gain_grad,
            second_shift_grad,
        ),
        ("batch", "head"),
    )
    delta_quad = attended_delta.reshape(block_shape)

    def block_grads(operands):
        query_blk, key_blk, value_blk, log_blk, delta_blk = operands
        scores = (
            jnp.einsum("qhe,hke->hqk", query_blk, key_blk, preferred_element_type=jnp.float32)
            * score_scale
        )
        probs = jnp.exp(scores - log_blk[..., None])
        value_part = jnp.einsum(
            "hqk,qhe->hke",
            probs.astype(jnp.bfloat16),
            delta_blk,
            preferred_element_type=jnp.float32,
        )
        prob_delta = jnp.einsum(
            "qhe,hke->hqk", delta_blk, value_blk, preferred_element_type=jnp.float32
        )
        row_inner = jnp.sum(probs * prob_delta, axis=-1, keepdims=True)
        score_delta = (probs * (prob_delta - row_inner)).astype(jnp.bfloat16)
        query_part = (
            jnp.einsum("hqk,hke->qhe", score_delta, key_blk, preferred_element_type=jnp.float32)
            * score_scale
        )
        key_part = (
            jnp.einsum("hqk,qhe->hke", score_delta, query_blk, preferred_element_type=jnp.float32)
            * score_scale
        )
        return (query_part, key_part, value_part)

    query_parts, key_parts, value_parts = lax.map(
        block_grads, (query_quad, key_sel, value_sel, log_totals, delta_quad)
    )
    zero_quad = jnp.zeros(block_shape, jnp.float32)
    query_delta = query_parts.reshape(all_rows, head_width).astype(jnp.bfloat16)
    key_delta = (
        zero_quad.at[chosen, :, head_ids, :]
        .add(key_parts)
        .reshape(all_rows, head_width)
        .astype(jnp.bfloat16)
    )
    value_delta = (
        zero_quad.at[chosen, :, head_ids, :]
        .add(value_parts)
        .reshape(all_rows, head_width)
        .astype(jnp.bfloat16)
    )
    query_weight_grad = product_tn(gathered, query_delta)
    key_weight_grad = product_tn(gathered, key_delta)
    value_weight_grad = product_tn(gathered, value_delta)
    query_bias_grad = jnp.sum(query_delta.astype(jnp.float32), axis=0)
    value_bias_grad = jnp.sum(value_delta.astype(jnp.float32), axis=0)
    token_part = lax.psum_scatter(
        (
            product_nt(query_delta, query_weight)
            + product_nt(key_delta, key_weight)
            + product_nt(value_delta, value_weight)
        ).astype(jnp.bfloat16),
        "head",
        scatter_dimension=0,
        tiled=True,
    ).astype(jnp.float32)
    tokens_grad = (token_part + mixed_delta).astype(jnp.bfloat16)
    weight_total = lax.psum(
        (
            query_weight_grad,
            key_weight_grad,
            value_weight_grad,
            query_bias_grad,
            value_bias_grad,
            mixer_share,
            expand_share,
            reduce_share,
        ),
        "batch",
    )
    query_sum, key_sum, value_sum, qbias_sum, vbias_sum, mixer_sum, expand_sum, reduce_sum = (
        weight_total
    )
    (
        mixer_bias_sum,
        first_gain_sum,
        first_shift_sum,
        expand_bias_sum,
        reduce_bias_sum,
        second_gain_sum,
        second_shift_sum,
    ) = vector_total
    return (
        layer_output.astype(jnp.bfloat16),
        tokens_grad,
        query_sum,
        key_sum,
        value_sum,
        qbias_sum,
        vbias_sum,
        mixer_sum,
        mixer_bias_sum,
        first_gain_sum,
        first_shift_sum,
        expand_sum,
        expand_bias_sum,
        reduce_sum,
        reduce_bias_sum,
        second_gain_sum,
        second_shift_sum,
    )


def solution(mesh):
    return jax.shard_map(
        per_device,
        mesh=mesh,
        in_specs=(
            P(("batch", "head"), None),
            P(None, "head"),
            P(None, "head"),
            P(None, "head"),
            P("head"),
            P("head"),
            P(),
            P(),
            P(),
            P(),
            P(),
            P(),
            P(),
            P(),
            P(),
            P(),
            P(("batch", "head"), None),
            P("batch"),
            P("batch", "head", None),
            P("batch", "head", None),
        ),
        out_specs=(
            P(("batch", "head"), None),
            P(("batch", "head"), None),
            P(None, "head"),
            P(None, "head"),
            P(None, "head"),
            P("head"),
            P("head"),
            P("head", None),
            P(),
            P(),
            P(),
            P(None, "head"),
            P(),
            P("head", None),
            P(),
            P(),
            P(),
        ),
        check_vma=False,
    )
```

profile of v0, /device:TPU:0, one launch (start us, length us, event | category | flops | bytes accessed | tf_op | source)
XLA Modules:
  0.0 654.7 jit_solution(16048121162065275175)
XLA Ops:
  12.3 89.5 %all-gather.2.cloned.1.call-done = bf16[3072,768]{1,0:T(8,128)(2,1)} async-done(((bf16[768,768]{1,0:T(8,128)(2,1)}), bf16[3072,768]{1,0:T(8,128)(2,1)}) %all-gather.2.cloned.1.call-update) | async-done | bytes 4718608 | tf_op jit(solution)/shard_map/all_gather | solution.py:91
  101.8 4.1 fusion.58
  105.9 2.3 reshape.384
  108.2 1.8 copy.96
  110.0 4.0 convolution_convert_fusion.2
  114.0 2.3 reshape.386
  118.1 1.8 gather_fusion.2
  120.5 4.0 fusion.59
  124.6 2.3 reshape.385
  128.6 25.0 %while.26 = (s32[]{:T(128)}, bf16[6,512,3,64]{1,3,2,0:T(8,128)(2,1)}, f32[6,3,512]{2,1,0:T(4,128)}, bf16[6,3,512,64]{2,3,1,0:T(8,128)(2,1)}, bf16[6,512,3,64]{1,...) while((s32[]{:T(128)}, bf16[6,512,3,64]{1,3,2,0:T(8,128)(2,1)}, ...), condition=%wide.region_3.4_spmd, body=%wide.region_0.3_spmd.sunk | while | flops 208501248 | bytes 10277453 | solution.py:114
  130.4 2.4 fusion.157
  134.6 2.4 fusion.157
  138.7 2.4 fusion.157
  142.9 2.4 fusion.157
  147.0 2.4 fusion.157
  151.2 2.4 fusion.157
  153.6 3.1 copy.99
  156.7 3.8 all_to_all.26
  160.5 2.4 copy.100
  162.9 4.3 all-to-all-start
  167.2 2.4 copy.101
  169.6 2.4 copy.103
  171.9 24.1 %all-to-all-done = bf16[4,768,192]{1,2,0:T(8,128)(2,1)} async-done(((bf16[4,768,192]{1,2,0:T(8,128)(2,1)}), bf16[4,768,192]{1,2,0:T(8,128)(2,1)}, u32[]{:S(2)}, u32[]{:S(2)}) %all-to-all-start) | async-done | bytes 1179680 | tf_op jit(solution)/shard_map/all_to_all | solution.py:117
  196.1 3.0 fusion.102
  200.9 28.5 %multiply_convert_fusion.1 = (bf16[768,3072]{1,0:T(8,128)(2,1)S(1)}, f32[768,3072]{1,0:T(8,128)}, f32[768,3072]{1,0:T(8,128)}) fusion(f32[3072]{0:T(1024)S(1)} %copy-done.25, bf16[768,3072]{1,0:T(8,128)(2,1)S(1)} %bitcast.212, f32[768,768]{0,1:T(8,128)S(1)} %get-tuple-element.271, f32[768]{0:T(1024)S(1)} %copy-done.28, f32[768]{0:T(1024)S(1)} %copy-done.24, ...), kind=kOutput, calls=%fused_computation.68 | convolution fusion | flops 3782541312 | bytes 30695424 | tf_op jit(solution)/shard_map/dot_general | solution.py:16
  229.4 4.8 fusion.103
  237.2 2.1 convert_reduce_fusion.2
  239.3 13.3 %convert_reduce_fusion = (f32[3072]{0:T(1024)}, bf16[768,3072]{1,0:T(8,128)(2,1)}) fusion(f32[768,3072]{1,0:T(8,128)} %get-tuple-element.262, f32[768,3072]{1,0:T(8,128)} %get-tuple-element.272, f32[3072]{0:T(1024)S(1)} %copy-done.25, bf16[768,768]{0,1:T(8,128)(2,1)S(1)} %get-tuple-element.254, bf16[3072,768]{1,0:T(8,128)(2,1)S(1)} %bitcast.210), kind=kOutput, calls=%fused_computation.65 | convolution fusion | flops 3663983616 | bytes 29515776 | tf_op jit(solution)/shard_map/dot_general | solution.py:26
  252.5 9.2 %multiply_reduce_fusion.2 = (f32[768]{0:T(1024)}, f32[768]{0:T(1024)S(1)}, f32[768]{0:T(1024)S(1)}, f32[768]{0:T(1024)}, f32[768,768]{0,1:T(8,128)S(1)}) fusion(f32[768,768]{0,1:T(8,128)S(1)} %get-tuple-element.271, f32[768]{0:T(1024)S(1)} %add_rsqrt_fusion.1, f32[768]{0:T(1024)S(1)} %broadcast_multiply_fusion.5, f32[768]{0:T(1024)S(1)} %copy-done.24, ...), kind=kOutput, calls=%fused_computation.100 | convolution fusion | flops 3634492416 | bytes 17731584 | tf_op jit(solution)/shard_map/dot_general | solution.py:26
  264.0 3.4 convolution_convert_fusion.4
  267.5 9.2 %convolution_convert_fusion.1 = bf16[768,3072]{1,0:T(8,128)(2,1)} fusion(bf16[768,3072]{1,0:T(8,128)(2,1)} %get-tuple-element.256, f32[768,768]{0,1:T(8,128)} %copy-done.11, f32[768]{0:T(1024)} %param.33, f32[768]{0:T(1024)} %param.32, f32[768]{0:T(1024)S(1)} %add_rsqrt_fusion.1, f32[768]{0:T(1024)S(1)} %broadcast_multiply_fusion.5), kind=kOutput, calls=%fused_computation.83 | convolution fusion | flops 3629187072 | bytes 11808768 | tf_op jit(solution)/shard_map/dot_general | solution.py:20
  276.7 3.8 convolution_convert_fusion.3
  280.5 4.4 all-to-all-start.1
  286.3 8.8 %convolution_convert_fusion = bf16[3072,768]{1,0:T(8,128)(2,1)} fusion(bf16[768,3072]{1,0:T(8,128)(2,1)} %copy-done.30, bf16[768,768]{0,1:T(8,128)(2,1)} %copy-done.13), kind=kOutput, calls=%fused_computation.82 | convolution fusion | flops 3626237952 | bytes 10616832 | tf_op jit(solution)/shard_map/dot_general | solution.py:20
  295.4 42.6 %all-to-all-done.1 = bf16[768,4,192]{0,2,1:T(8,128)(2,1)} async-done(((bf16[768,4,192]{0,2,1:T(8,128)(2,1)}), bf16[768,4,192]{0,2,1:T(8,128)(2,1)}, u32[]{:S(2)}, u32[]{:S(2)}) %all-to-all-start.1) | async-done | bytes 1179680 | tf_op jit(solution)/shard_map/all_to_all | solution.py:148
  338.0 3.2 copy.105
  341.1 3.7 reshape.387
  344.8 2.8 copy.107
  347.7 52.7 %while.27 = (s32[]{:T(128)}, bf16[6,512,3,64]{1,3,2,0:T(8,128)(2,1)}, f32[6,3,512,64]{2,3,1,0:T(8,128)}, f32[6,3,512,64]{2,3,1,0:T(8,128)}, bf16[6,3,512,64]{2,3...) while((s32[]{:T(128)}, ...), condition=%wide.region_14.15_spmd, body=%wide.region_12.14_spmd.sunk | while | flops 512948736 | bytes 26197096 | solution.py:202
  349.0 1.8 multiply_reduce_fusion.10
  354.1 2.3 fusion.169
  357.8 1.9 multiply_reduce_fusion.10
  362.9 2.3 fusion.169
  366.5 1.8 multiply_reduce_fusion.10
  371.6 2.3 fusion.169
  375.3 1.8 multiply_reduce_fusion.10
  380.4 2.3 fusion.169
  384.1 1.8 multiply_reduce_fusion.10
  389.2 2.3 fusion.169
  392.9 1.8 multiply_reduce_fusion.10
  398.0 2.3 fusion.169
  400.6 6.4 scatter_fusion.1
  410.3 6.6 %scatter_fusion = f32[6,512,3,64]{1,3,2,0:T(8,128)S(1)} fusion(f32[6,512,3,64]{1,3,2,0:T(8,128)S(1)} %broadcast.563.clone, s32[18]{0:T(128)S(1)} %reshape.412, f32[18,512,64]{1,2,0:T(8,128)} %bitcast.204), kind=kCustom, calls=%fused_computation.4 | custom fusion | flops 589824 | bytes 7078032 | tf_op jit(solution)/shard_map/scatter-add | solution.py:209
  422.5 5.2 add_convert_fusion
  429.0 4.2 convolution_bitcast_fusion
  433.2 4.3 convolution_bitcast_fusion.1
  437.5 4.4 convolution_bitcast_fusion.2
  443.4 45.0 %all-reduce = (f32[768]{0:T(1024)}, f32[768]{0:T(1024)}, f32[768]{0:T(1024)}, f32[3072]{0:T(1024)}, f32[768]{0:T(1024)}, /*index=5*/f32[768]{0:T(1024)}, f32[768]{0:T(1024)}) all-reduce(f32[768]{0:T(1024)S(1)} %get-tuple-element.257, f32[768]{0:T(1024)} %get-tuple-element.200, ...), channel_id=1, replica_groups=mesh['batch'=8,'head'=4] {'batch','head'}, use_global_device_ids=true, to_apply=%region_28.29 | all-reduce | flops 7680 | bytes 61440 | tf_op jit(solution)/shard_map/psum | solution.py:160
  489.5 117.9 %all-reduce.7 = (f32[192]{0:T(256)}, f32[192]{0:T(256)}, f32[192,768]{1,0:T(8,128)}, f32[768,768]{1,0:T(8,128)}, f32[768,768]{1,0:T(8,128)}) all-reduce(f32[192]{0:T(256)S(1)} %reduce_sum.184, f32[192]{0:T(256)S(1)} %reduce_sum.186, ...), channel_id=1, replica_groups=mesh['batch'=8,'head'=4] {'batch'}, use_global_device_ids=true, to_apply=%region_22.23 | all-reduce | flops 1327488 | bytes 7965696 | tf_op jit(solution)/shard_map/psum | solution.py:235
  607.4 2.5 add_convert_fusion.2
  609.9 2.4 copy.116
  612.3 30.4 %all-reduce.6.cloned.1.call-done = (f32[768,192]{0,1:T(8,128)}, f32[768,192]{0,1:T(8,128)}, f32[768,192]{0,1:T(8,128)}) async-done(((f32[768,192]{0,1:T(8,128)}, f32[768,192]{0,1:T(8,128)}, f32[768,192]{0,1:T(8,128)}), (f32[768,192]{0,1:T(8,128)}, f32[768,192]{0,1:T(8,128)}, f32[768,192]{0,1:T(8,128)})) %all-reduce.6.cloned.1.call-update) | async-done | bytes 1769488 | tf_op jit(solution)/shard_map/psum | solution.py:235
  642.7 2.0 copy.171
  644.7 1.9 copy.172
  (186 shorter events, 69.1 us)
Async XLA Ops:
  7.2 188.9 %copy-start = (bf16[768,768]{1,0:T(8,128)(2,1)S(1)}, bf16[768,768]{1,0:T(8,128)(2,1)}, u32[]{:S(2)}) copy-start(bf16[768,768]{1,0:T(8,128)(2,1)} %param.30) | copy-start | bytes 3538948
  7.2 94.5 %all-gather.2.cloned.1.call-start = ((), (), s32[]{:S(2)}) async-start(), calls=%async_computation.6 | async-start | bytes 5898240 | tf_op jit(solution)/shard_map/all_gather | solution.py:91
  108.2 1.8 copy-start.15
  119.8 0.7 copy-start.29
  162.9 33.2 %all-to-all-start = ((bf16[4,768,192]{1,2,0:T(8,128)(2,1)}), bf16[4,768,192]{1,2,0:T(8,128)(2,1)}, u32[]{:S(2)}, u32[]{:S(2)}) async-start(bf16[4,768,192]{1,2,0:T(8,128)(2,1)} %copy.100), calls=%async_computation | async-start | bytes 2359296 | tf_op jit(solution)/shard_map/all_to_all | solution.py:117
  167.1 29.0 %copy-start.26 = (f32[768]{0:T(1024)S(1)}, f32[768]{0:T(1024)}, u32[]{:S(2)}) copy-start(f32[768]{0:T(1024)} %param.31) | copy-start | bytes 9220
  167.1 322.3 %reduce-scatter.7.cloned.1.call-start = ((), (), s32[]{:S(2)}) async-start(), calls=%async_computation.8 | async-start | bytes 1474560 | tf_op jit(solution)/shard_map/reduce_scatter | solution.py:156
  196.1 3.4 slice-start.2
  196.1 3.4 slice-start.3
  196.1 33.3 %slice-start = ((s8[4718592]{0:T(1024)(128)(4,1)}), s8[4194304]{0:T(1024)(128)(4,1)S(1)}, s32[]{:S(2)}) async-start(s8[4718592]{0:T(1024)(128)(4,1)} %bitcast.209), calls=%async_computation.12 | async-start | bytes 8388608
  199.1 62.6 %copy-start.11 = (f32[768,768]{0,1:T(8,128)}, f32[768,768]{0,1:T(8,128)S(1)}, u32[]{:S(2)}) copy-start(f32[768,768]{0,1:T(8,128)S(1)} %get-tuple-element.271) | copy-start | bytes 7077892
  199.2 1.6 copy-start.24
  199.2 1.6 copy-start.25
  199.2 1.7 copy-start.28
  200.9 28.5 %slice-start.1 = ((s8[4718592]{0:T(1024)(128)(4,1)}), s8[524288]{0:T(1024)(128)(4,1)S(1)}, s32[]{:S(2)}) async-start(s8[4718592]{0:T(1024)(128)(4,1)} %bitcast.209), calls=%async_computation.13 | async-start | bytes 1048576
  200.9 28.6 %copy-start.27 = (f32[768]{0:T(1024)S(1)}, f32[768]{0:T(1024)}, u32[]{:S(2)}) copy-start(f32[768]{0:T(1024)} %param.37) | copy-start | bytes 9220
  229.4 4.9 copy-start.30
  234.3 1.3 copy-start.6
  234.3 1.3 copy-start.19
  234.6 2.6 copy-start.23
  239.3 13.3 %copy-start.13 = (bf16[768,768]{0,1:T(8,128)(2,1)}, bf16[768,768]{0,1:T(8,128)(2,1)S(1)}, u32[]{:S(2)}) copy-start(bf16[768,768]{0,1:T(8,128)(2,1)S(1)} %get-tuple-element.254) | copy-start | bytes 3538948
  262.6 1.4 copy-start.9
  267.5 222.0 %reduce-scatter.9.cloned.1.call-start = ((), (), s32[]{:S(2)}) async-start(), calls=%async_computation.9 | async-start | bytes 5898240 | tf_op jit(solution)/shard_map/reduce_scatter | solution.py:150
  280.5 4.5 copy-start.22
  280.5 57.5 %all-to-all-start.1 = ((bf16[768,4,192]{0,2,1:T(8,128)(2,1)}), bf16[768,4,192]{0,2,1:T(8,128)(2,1)}, u32[]{:S(2)}, u32[]{:S(2)}) async-start(bf16[768,4,192]{0,2,1:T(8,128)(2,1)} %bitcast.208), calls=%async_computation.1 | async-start | bytes 2359296 | tf_op jit(solution)/shard_map/all_to_all | solution.py:148
  284.9 204.6 %reduce-scatter.11.cloned.1.call-start = ((), (), s32[]{:S(2)}) async-start(), calls=%async_computation.10 | async-start | bytes 5898240 | tf_op jit(solution)/shard_map/reduce_scatter | solution.py:153
  295.1 312.3 %reduce-scatter.5.cloned.1.call-start = ((), (), s32[]{:S(2)}) async-start(), calls=%async_computation.7 | async-start | bytes 5898240 | tf_op jit(solution)/shard_map/reduce_scatter | solution.py:224
  417.1 1.3 copy-start.7
  418.2 1.3 copy-start.1
  418.3 1.2 copy-start.16
  419.5 1.5 copy-start.3
  419.5 1.5 copy-start.17
  421.0 1.5 copy-start.18
  427.7 1.3 copy-start.5
  427.7 5.5 copy-start.2
  427.7 215.0 %all-reduce.6.cloned.1.call-start = ((), (), s32[]{:S(2)}) async-start(), calls=%async_computation.11 | async-start | bytes 3538944 | tf_op jit(solution)/shard_map/psum | solution.py:235
  433.2 4.3 copy-start.4
  437.5 4.4 copy-start.12
  441.9 1.5 copy-start.20
  441.9 1.5 copy-start.21
  441.9 47.2 %copy-start.8 = (bf16[6,512,3,64]{1,3,2,0:T(8,128)(2,1)S(1)}, bf16[6,512,3,64]{1,3,2,0:T(8,128)(2,1)}, u32[]{:S(2)}) copy-start(bf16[6,512,3,64]{1,3,2,0:T(8,128)(2,1)} %get-tuple-element.101) | copy-start | bytes 3538948
  489.4 118.0 %copy-start.10 = (f32[768,768]{0,1:T(8,128)S(1)}, f32[768,768]{0,1:T(8,128)}, u32[]{:S(2)}) copy-start(f32[768,768]{0,1:T(8,128)} %copy-done.9) | copy-start | bytes 7077892
  642.7 3.9 copy-start.14
Sparse Core Ops, SparseCore 0:
  9.6 92.0 all-gather.1
  267.6 35.8 reduce-scatter.6
  305.8 89.9 reduce-scatter.8
  398.0 86.6 reduce-scatter.10
  486.8 85.6 reduce-scatter.4
  576.5 66.1 all-reduce.5
where the time goes:
time: 666 us; the launch traced here: 655 us
  waiting for transfers between devices  187 us (28%)
  matrix products  178 us (27%)
  blocking collectives  163 us (24%)
  local copies, waits for them, and re-layouts  65.3 us (10%)
  other arithmetic  35.8 us (5%)
  between operations  15.7 us (2%)
  starting transfers between devices  9.1 us (1%)
    psum x1, blocking collectives, per_device(): lax.psum((query_weight_grad, key_weight_grad, value_weight_grad, query_bi...  118 us
    all_gather x1, waiting for transfers between devices, per_device(): gathered = lax.all_gather(tokens, 'head', axis=0, tiled=True)  89.5 us
    dot_general x6, matrix products, product(): return jnp.dot(matrix_a, matrix_b, preferred_element_type=jnp.float32)  48.5 us
    psum x1, blocking collectives, per_device(): lax.psum((mixer_bias_grad, first_gain_grad, first_shift_grad, expand_bias...  45 us
    all_to_all x1, waiting for transfers between devices, per_device(): lax.all_to_all(attended_back, 'head', split_axis=1, concat_axis=0, tiled=...  42.6 us
    dot_general x6, matrix products, product_nt(): lax.dot_general(matrix_a, matrix_b, (((1,), (1,)), ((), ())), preferred_e...  34.3 us
    dot_general x6, matrix products, product_tn(): lax.dot_general(matrix_a, matrix_b, (((0,), (0,)), ((), ())), preferred_e...  34.3 us
    psum x1, waiting for transfers between devices, per_device(): lax.psum((query_weight_grad, key_weight_grad, value_weight_grad, query_bi...  30.4 us
  transfers between devices with their start and end apart: 8, of which 4 were waited for; matrix products, arithmetic and copies ran while one was open for 22% of the time, Pallas kernels for 0%

commit v1 on v0

v1 whole, which is shorter than its diff:
```python
import functools
import math

import jax
import jax.numpy as jnp
from jax import lax
from jax.experimental import pallas as pl
from jax.experimental.pallas import tpu as pltpu
from jax.sharding import PartitionSpec as P

MESH = pl.DeviceIdType.MESH
BF = jnp.bfloat16
F32 = jnp.float32
VMEM_LIMIT = 60 * 2**20

D = 768
HEAD_SIZE = 64
BLOCK = 512
ROWS = 768
TILE = 256
WINDOW = 2048
SLOT = 192
FF = 3072
EPSILON = 1e-05
SCALE = 1.0 / math.sqrt(HEAD_SIZE)
EXP2_SCALE = SCALE * math.log2(math.e)
CHUNKS = 6


def dot_nn(a, b):
    return lax.dot_general(a, b, (((1,), (0,)), ((), ())), preferred_element_type=F32)


def dot_nt(a, b):
    return lax.dot_general(a, b, (((1,), (1,)), ((), ())), preferred_element_type=F32)


def dot_tn(a, b):
    return lax.dot_general(a, b, (((0,), (0,)), ((), ())), preferred_element_type=F32)


def remote(src, dst, send, recv, b, h):
    return pltpu.make_async_remote_copy(
        src_ref=src, dst_ref=dst, send_sem=send, recv_sem=recv, device_id=(b, h), device_id_type=MESH
    )


def flip(b, step):
    return b + step - 2 * step * ((b // step) % 2)


def own_offset(h):
    return pl.multiple_of(768 * h - 1024 * (h // 2), 256)


def start_kernel(
    tok, wq, wk, wv, qb, vb, pairs, triples,
    xw, wt, qbs, vbs, pairs_all, triples_all,
    tok_v, w_v, loc, send, recv,
):
    b = lax.axis_index("batch")
    h = lax.axis_index("head")
    core = b % 2
    pc, px, py = flip(b, 1), flip(b, 2), flip(b, 4)
    hp = flip(h, 1)
    hm = 3 - h
    middle = jnp.logical_or(h == 1, h == 2)
    others = [(h + d) % 4 for d in (1, 2, 3)]
    barrier = pltpu.get_barrier_semaphore()
    for target in [(pc, h), (px, h), (py, h)] + [(b, o) for o in others]:
        pl.semaphore_signal(barrier, inc=1, device_id=target, device_id_type=MESH)

    own = own_offset(h)
    small = ((qb, qbs), (vb, vbs), (pairs, pairs_all), (triples, triples_all))
    weights = (wq, wk, wv)
    fetch = [(tok, tok_v)] + [(src, w_v.at[m]) for m, src in enumerate(weights)]
    fetch = [pltpu.make_async_copy(src, dst, loc.at[i]) for i, (src, dst) in enumerate(fetch)]
    kept = [(tok_v, xw.at[pl.ds(own, ROWS)])]
    kept += [(w_v.at[m], wt.at[h, m]) for m in range(3)]
    kept += [(src, dst.at[h]) for src, dst in small]
    kept = [pltpu.make_async_copy(src, dst, loc.at[4 + i]) for i, (src, dst) in enumerate(kept)]
    fill = pltpu.make_async_copy(
        tok_v.at[pl.ds(0, BLOCK)],
        xw.at[pl.ds(pl.multiple_of(1536 - 512 * h, 256), BLOCK)],
        loc.at[12],
    )
    for c in fetch + kept[4:]:
        c.start()
    pl.semaphore_wait(barrier, 6)

    def piece(who):
        return pl.ds(pl.multiple_of(((who // 2) % 4) * 48, 16), 48)

    lanes = pl.ds(pl.multiple_of(core * 384, 128), 384)
    sem = iter(range(128))

    def make(src, dst, who, where):
        i = next(sem)
        c = remote(src, dst, send.at[i], recv.at[i], who, where)
        return c

    mine = piece(b)
    near = (1, 3, 2)
    over_z = {}
    for d in near:
        for m, src in enumerate(weights):
            c = make(src.at[mine, lanes], wt.at[h, m, mine, lanes], b, others[d - 1])
            c.start()
            over_z[d, m] = c
    tables = []
    for src, dst in small:
        for d in near:
            c = make(src, dst.at[h], b, others[d - 1])
            c.start()
            tables.append(c)
    pair = make(tok, xw.at[pl.ds(own, ROWS)], b, hp)
    cross = make(
        tok.at[pl.ds(pl.multiple_of(256 * (h % 2), 256), BLOCK)],
        xw.at[pl.ds(pl.multiple_of(1536 * ((h + 1) % 2), 256), BLOCK)],
        b,
        hm,
    )

    for i, c in enumerate(fetch):
        c.wait()
        kept[i].start()

    @pl.when(jnp.logical_not(middle))
    def _():
        fill.start()

    def forward(d, m, rows, who):
        slot = (h + 4 - d) % 4
        ref = wt.at[slot, m, rows, lanes]
        c = make(ref, ref, who, h)
        c.start()
        return c

    units = [(d, m) for d in near for m in range(3)]
    first = {}
    for i, (d, m) in enumerate(units):
        over_z[d, m].wait()
        first[d, m] = forward(d, m, mine, px if i % 2 == 0 else py)
        if i == 5:
            pair.start()

            @pl.when(middle)
            def _():
                cross.start()

    second = {}
    for i, (d, m) in enumerate(units):
        first[d, m].wait()
        came, go = (px, py) if i % 2 == 0 else (py, px)
        second[d, m] = [forward(d, m, mine, go), forward(d, m, piece(came), go)]
    third = {}
    for d, m in units:
        for c in second[d, m]:
            c.wait()
        third[d, m] = forward(d, m, slice(None), pc)
    for c in third.values():
        c.wait()
    for c in tables:
        c.wait()
    pair.wait()
    for c in kept:
        c.wait()

    @pl.when(middle)
    def _():
        cross.wait()

    @pl.when(jnp.logical_not(middle))
    def _():
        fill.wait()


def start_exchange(*args):
    hb = pl.BlockSpec(memory_space=pl.ANY)
    qb, pairs, triples = args[4], args[6], args[7]
    return pl.pallas_call(
        start_kernel,
        out_shape=(
            jax.ShapeDtypeStruct((WINDOW, D), BF),
            jax.ShapeDtypeStruct((4, 3, SLOT, D), BF),
            jax.ShapeDtypeStruct((4,) + qb.shape, F32),
            jax.ShapeDtypeStruct((4,) + qb.shape, F32),
            jax.ShapeDtypeStruct((4,) + pairs.shape, jnp.int32),
            jax.ShapeDtypeStruct((4,) + triples.shape, jnp.int32),
        ),
        in_specs=[hb] * 8,
        out_specs=(hb,) * 6,
        scratch_shapes=[
            pltpu.VMEM((ROWS, D), BF),
            pltpu.VMEM((3, SLOT, D), BF),
            pltpu.SemaphoreType.DMA((13,)),
            pltpu.SemaphoreType.DMA((60,)),
            pltpu.SemaphoreType.DMA((60,)),
        ],
        compiler_params=pltpu.CompilerParams(
            collective_id=0, has_side_effects=True, vmem_limit_bytes=VMEM_LIMIT
        ),
        name="start_exchange",
    )(*args)


def key_index(kinds, pairs, triples, h, tile, head):
    block = (3 * h + tile) // 2
    slot, local = head // 3, head % 3
    pair_pick = 2 * (block // 2) + pairs[slot, block // 2, block % 2, local]
    triple_pick = 3 * (block // 3) + triples[slot, local, block // 3, block % 3]
    chosen = jnp.where(kinds[0] == 0, pair_pick, triple_pick)
    return pl.multiple_of((chosen - 2 * (h // 2)) * BLOCK, BLOCK)


def left_lanes(rows):
    return lax.broadcasted_iota(jnp.int32, (rows, 128), 1) < 64


def attend_kernel(
    kinds, pairs, triples, qbs, vbs, xw, wt,
    p_out, att_out, inv_out, q_out, ks_out, vs_out, mask_out,
    x_v, w_v, q_v, k_v, v_v, sems,
):
    g, t = pl.program_id(0), pl.program_id(1)
    h = lax.axis_index("head")

    @pl.when(jnp.logical_and(g == 0, t == 0))
    def _():
        loads = [pltpu.make_async_copy(wt, w_v, sems.at[0])]
        for c in range(4):
            part = pl.ds(512 * c, 512)
            loads.append(pltpu.make_async_copy(xw.at[part], x_v.at[part], sems.at[1 + c]))
        for c in loads:
            c.start()
        q_bias = jnp.concatenate([qbs[s] for s in range(4)], axis=1)
        v_bias = jnp.concatenate([vbs[s] for s in range(4)], axis=1)
        for c in loads:
            c.wait()
        w_q = w_v[:, 0].reshape(D, D)
        w_k = w_v[:, 1].reshape(D, D)
        w_v2 = w_v[:, 2].reshape(D, D)

        @pl.loop(0, 4)
        def _(c):
            at = pl.ds(pl.multiple_of(c * 512, 512), 512)
            x = x_v[at, :]
            k = dot_nt(x, w_k).astype(BF)
            v = (dot_nt(x, w_v2) + v_bias).astype(BF)
            for s in range(3):
                k_v[s, at, :] = k[:, 256 * s : 256 * s + 256]
                v_v[s, at, :] = v[:, 256 * s : 256 * s + 256]

        own = own_offset(h)

        @pl.loop(0, 3)
        def _(c):
            x = x_v[pl.ds(pl.multiple_of(own + c * TILE, TILE), TILE), :]
            q = (dot_nt(x, w_q) + q_bias).astype(BF)
            for s in range(3):
                q_v[s, pl.ds(pl.multiple_of(c * TILE, TILE), TILE), :] = q[:, 256 * s : 256 * s + 256]

    left = left_lanes(TILE)
    left_keys = left_lanes(BLOCK)
    lane_head = lax.broadcasted_iota(jnp.int32, (8, 256), 1) // 64
    key_block = lax.broadcasted_iota(jnp.int32, (8, 256), 0)
    mask_rows = jnp.zeros((8, 256), F32)
    for pair in range(2):
        at = slice(128 * pair, 128 * pair + 128)
        q = q_v[g, pl.ds(pl.multiple_of(t * TILE, TILE), TILE), at]
        q_out[:, at] = q
        found, picked = [], []
        for side in range(2):
            mask = left if side == 0 else jnp.logical_not(left)
            mask_keys = left_keys if side == 0 else jnp.logical_not(left_keys)
            row = key_index(kinds, pairs, triples, h, t, 4 * g + 2 * pair + side)
            keys = k_v[g, pl.ds(row, BLOCK), at]
            values = v_v[g, pl.ds(row, BLOCK), at]
            picked.append((keys, values))
            here = jnp.logical_and(lane_head == 2 * pair + side, key_block == row // BLOCK)
            mask_rows = jnp.where(here, 1.0, mask_rows)
            scores = dot_nt(jnp.where(mask, q, jnp.zeros_like(q)), keys)
            top = jnp.max(scores, axis=-1, keepdims=True)
            raised = jnp.exp2((scores - top) * EXP2_SCALE).astype(BF)
            p_out[0, 2 * pair + side] = raised
            found.append(dot_nn(raised, jnp.where(mask_keys, values, jnp.ones_like(values))))
        result = jnp.where(left, found[0], found[1])
        total = jnp.where(left, found[1], found[0])
        inverse = 1.0 / pltpu.roll(total, 64, 1)
        att_out[:, at] = (result * inverse).astype(BF)
        inv_out[:, at] = inverse
        ks_out[0, :, at] = jnp.where(left_keys, picked[0][0], picked[1][0])
        vs_out[0, :, at] = jnp.where(left_keys, picked[0][1], picked[1][1])
    mask_out[0] = mask_rows


def attend(kinds, pairs, triples, qbs, vbs, xw, wt):
    hb = pl.BlockSpec(memory_space=pl.ANY)
    sm = pl.BlockSpec(memory_space=pltpu.SMEM)
    vm = pl.BlockSpec(memory_space=pltpu.VMEM)
    tile = pl.BlockSpec((TILE, 256), lambda g, t: (t, g))
    picked = pl.BlockSpec((1, BLOCK, 256), lambda g, t: (3 * g + t, 0, 0))
    return pl.pallas_call(
        attend_kernel,
        grid=(3, 3),
        out_shape=(
            jax.ShapeDtypeStruct((9, 4, TILE, BLOCK), BF),
            jax.ShapeDtypeStruct((ROWS, D), BF),
            jax.ShapeDtypeStruct((ROWS, D), F32),
            jax.ShapeDtypeStruct((ROWS, D), BF),
            jax.ShapeDtypeStruct((9, BLOCK, 256), BF),
            jax.ShapeDtypeStruct((9, BLOCK, 256), BF),
            jax.ShapeDtypeStruct((3, 8, D), F32),
        ),
        in_specs=[sm, sm, sm, vm, vm, hb, hb],
        out_specs=(
            pl.BlockSpec((1, 4, TILE, BLOCK), lambda g, t: (3 * g + t, 0, 0, 0)),
            tile,
            tile,
            tile,
            picked,
            picked,
            pl.BlockSpec((1, 8, 256), lambda g, t: (t, 0, g)),
        ),
        scratch_shapes=[
            pltpu.VMEM((WINDOW, D), BF),
            pltpu.VMEM((4, 3, SLOT, D), BF),
            pltpu.VMEM((3, ROWS, 256), BF),
            pltpu.VMEM((3, WINDOW, 256), BF),
            pltpu.VMEM((3, WINDOW, 256), BF),
            pltpu.SemaphoreType.DMA((8,)),
        ],
        compiler_params=pltpu.CompilerParams(
            dimension_semantics=("arbitrary", "arbitrary"), vmem_limit_bytes=VMEM_LIMIT
        ),
        name="attend",
    )(kinds, pairs, triples, qbs, vbs, xw, wt)


def normal_parts(v):
    bell = jnp.exp2(v * v * (-0.5 * math.log2(math.e)))
    t = 1.0 / (1.0 + (0.3275911 / math.sqrt(2.0)) * jnp.abs(v))
    poly = 0.5 * 1.061405429
    poly = poly * t + 0.5 * -1.453152027
    poly = poly * t + 0.5 * 1.421413741
    poly = poly * t + 0.5 * -0.284496736
    poly = poly * t + 0.5 * 0.254829592
    tail = poly * t * bell
    phi_sum = jnp.where(v >= 0, 1.0 - tail, tail)
    return phi_sum, bell * (1.0 / math.sqrt(2.0 * math.pi))


def norm_parts(values):
    center = values - jnp.mean(values, axis=-1, keepdims=True)
    inverse = lax.rsqrt(jnp.mean(center * center, axis=-1, keepdims=True) + EPSILON)
    return center * inverse, inverse


def norm_back(inner, scaled, inverse):
    inner_mean = jnp.mean(inner, axis=-1, keepdims=True)
    cross_mean = jnp.mean(inner * scaled, axis=-1, keepdims=True)
    return inverse * (inner - inner_mean - scaled * cross_mean)


def column_sum(values):
    return jnp.sum(values, axis=0, keepdims=True)


def dense_kernel(
    att_h, tok_h, cot_h, mw_h, ew_h, rw_h, inv_h, mb, g1, s1, rb, g2, s2, eb,
    out_o, mixed_o, delta_o, low, rdel, mdel, act_h, hdel_h, sums_o,
    att, tok, cot, mw, ew, rw, inv, act, slope, hdel, sems,
):
    loads = [
        pltpu.make_async_copy(src, dst, sems.at[i])
        for i, (src, dst) in enumerate(
            ((att_h, att), (mw_h, mw), (tok_h, tok), (ew_h, ew), (rw_h, rw), (cot_h, cot), (inv_h, inv))
        )
    ]
    for c in loads:
        c.start()
    sums_o[...] = jnp.zeros_like(sums_o)
    for c in loads:
        c.wait()

    @pl.loop(0, 3)
    def _(t):
        at = pl.ds(pl.multiple_of(t * TILE, TILE), TILE)
        mixed = dot_nn(att[at, :], mw[...]) + mb[...] + tok[at, :].astype(F32)
        scaled_one, inverse_one = norm_parts(mixed)
        normed = scaled_one * g1[...] + s1[...]
        normed_low = normed.astype(BF)
        low[at, :] = normed_low
        branch = rb[...] + normed
        for j in range(4):
            cols = slice(768 * j, 768 * j + 768)
            hidden = dot_nn(normed_low, ew[:, cols]) + eb[:, cols]
            phi_sum, bell = normal_parts(hidden)
            active = (hidden * phi_sum).astype(BF)
            act[j, at, :] = active
            slope[:, cols] = (phi_sum + hidden * bell).astype(BF)
            branch += dot_nn(active, rw[cols, :])
        scaled_two, inverse_two = norm_parts(branch)
        out_o[at, :] = (scaled_two * g2[...] + s2[...]).astype(BF)
        upstream = cot[at, :].astype(F32)
        sums_o[4:5, :] += column_sum(upstream * scaled_two)
        sums_o[5:6, :] += column_sum(upstream)
        branch_delta = norm_back(upstream * g2[...], scaled_two, inverse_two)
        reduce_delta = branch_delta.astype(BF)
        rdel[at, :] = reduce_delta
        sums_o[3:4, :] += column_sum(reduce_delta.astype(F32))
        normed_delta = branch_delta
        for j in range(4):
            cols = slice(768 * j, 768 * j + 768)
            back = dot_nt(reduce_delta, rw[cols, :]) * slope[:, cols].astype(F32)
            back_low = back.astype(BF)
            hdel[j, at, :] = back_low
            sums_o[6 + j : 7 + j, :] += column_sum(back_low.astype(F32))
            normed_delta += dot_nt(back_low, ew[:, cols])
        sums_o[1:2, :] += column_sum(normed_delta * scaled_one)
        sums_o[2:3, :] += column_sum(normed_delta)
        mixed_delta = norm_back(normed_delta * g1[...], scaled_one, inverse_one)
        mixed_o[at, :] = mixed_delta
        mixer_delta = mixed_delta.astype(BF)
        mdel[at, :] = mixer_delta
        sums_o[0:1, :] += column_sum(mixer_delta.astype(F32))
        delta_o[at, :] = (dot_nt(mixer_delta, mw[...]) * inv[at, :]).astype(BF)
        pltpu.make_async_copy(act.at[:, at], act_h.at[:, at], sems.at[7 + t]).start()
        pltpu.make_async_copy(hdel.at[:, at], hdel_h.at[:, at], sems.at[10 + t]).start()

    for t in range(3):
        at = pl.ds(t * TILE, TILE)
        pltpu.make_async_copy(act.at[:, at], act_h.at[:, at], sems.at[7 + t]).wait()
        pltpu.make_async_copy(hdel.at[:, at], hdel_h.at[:, at], sems.at[10 + t]).wait()


def dense(*args):
    hb = pl.BlockSpec(memory_space=pl.ANY)
    vm = pl.BlockSpec(memory_space=pltpu.VMEM)
    rows = jax.ShapeDtypeStruct((ROWS, D), BF)
    wide = jax.ShapeDtypeStruct((4, ROWS, D), BF)
    return pl.pallas_call(
        dense_kernel,
        out_shape=(
            rows,
            jax.ShapeDtypeStruct((ROWS, D), F32),
            rows,
            rows,
            rows,
            rows,
            wide,
            wide,
            jax.ShapeDtypeStruct((16, D), F32),
        ),
        in_specs=[hb] * 7 + [vm] * 7,
        out_specs=(vm,) * 6 + (hb, hb, vm),
        scratch_shapes=[
            pltpu.VMEM((ROWS, D), BF),
            pltpu.VMEM((ROWS, D), BF),
            pltpu.VMEM((ROWS, D), BF),
            pltpu.VMEM((D, D), BF),
            pltpu.VMEM((D, FF), BF),
            pltpu.VMEM((FF, D), BF),
            pltpu.VMEM((ROWS, D), F32),
            pltpu.VMEM((4, ROWS, D), BF),
            pltpu.VMEM((TILE, FF), BF),
            pltpu.VMEM((4, ROWS, D), BF),
            pltpu.SemaphoreType.DMA((13,)),
        ],
        compiler_params=pltpu.CompilerParams(vmem_limit_bytes=VMEM_LIMIT),
        name="dense",
    )(*args)


def finish_kernel(
    nb, act_h, hdel_h, low_h, rdel_h, att_h, mdel_h, p_h, ks_h, vs_h, q_h, delta_h, xw_h, wt_h, mixed_h, masks, sums_in,
    res_h, tg_o, sums_o, from_more,
    stage, from_core, from_a, from_b, from_z, res, dx_pair, dx_mid, vec, vec_in,
    wide_a, wide_b, four, dv_low, own, p_v, ks_v, vs_v, q_v, d_v, a_v, dx_v, mid_v, own_v, loc, flow, send, recv,
):
    b = lax.axis_index("batch")
    h = lax.axis_index("head")
    core, xb, yb = b % 2, (b // 2) % 2, (b // 4) % 2
    pc, px, py = flip(b, 1), flip(b, 2), flip(b, 4)
    hp, hm, hq = flip(h, 1), 3 - h, flip(h, 2)
    middle = jnp.logical_or(h == 1, h == 2)
    others = [(h + d) % 4 for d in (1, 2, 3)]
    more = []
    step = 8
    while step < nb:
        more.append(flip(b, step))
        step *= 2
    barrier = pltpu.get_barrier_semaphore()
    targets = [(pc, h), (px, h), (py, h)] + [(m, h) for m in more] + [(b, o) for o in others]
    for target in targets:
        pl.semaphore_signal(barrier, inc=1, device_id=target, device_id_type=MESH)

    def local(i, src, dst):
        return pltpu.make_async_copy(src, dst, loc.at[i])

    loads = [
        local(0, act_h, wide_a),
        local(1, rdel_h, four.at[1]),
        local(2, low_h, four.at[0]),
        local(3, hdel_h, wide_b),
        local(4, att_h, four.at[2]),
        local(5, mdel_h, four.at[3]),
        local(6, mixed_h, own),
    ]
    for c in loads[:2]:
        c.start()

    def make(i, src, dst, who, where):
        return remote(src, dst, send.at[i], recv.at[i], who, where)

    bits = ((xb, px, yb, py), (yb, py, xb, px))
    columns = (pl.ds(0, 384), pl.ds(384, 384))

    def rows_of(start, count):
        return pl.ds(pl.multiple_of(start, 16), count)

    def place_start(part, level):
        start = core * 192
        if level < 2:
            start = start + bits[part][0] * 96
        if level < 1:
            start = start + bits[part][2] * 48
        return start

    def place(part, level):
        return rows_of(place_start(part, level), (48, 96, 192)[level])

    def core_copy(k):
        return make(k, stage.at[k % 4, :, rows_of((1 - core) * 192, 192)], from_core.at[k], pc, h)

    def a_copy(k, part):
        a_bit, who = bits[part][:2]
        src = stage.at[k % 4, :, rows_of(core * 192 + (1 - a_bit) * 96, 96), columns[part]]
        return make(6 + 2 * k + part, src, from_a.at[k, :, :, columns[part]], who, h)

    def b_copy(k, part):
        a_bit, _, b_bit, who = bits[part]
        src = stage.at[k % 4, :, rows_of(core * 192 + a_bit * 96 + (1 - b_bit) * 48, 48), columns[part]]
        return make(18 + 2 * k + part, src, from_b.at[k, :, :, columns[part]], who, h)

    def z_copy(k, part, d):
        o = others[d - 1]
        src = stage.at[k % 4, o, place(part, 0), columns[part]]
        return make(30 + 6 * k + 3 * part + d - 1, src, from_z.at[k, d - 1, :, columns[part]], b, o)

    def gather_copy(k, part, level):
        ref = res.at[k, place(part, level), columns[part]]
        return make(66 + 12 * level + 2 * k + part, ref, ref, bits[part][3 if level == 0 else 1], h)

    def last_copy(k):
        ref = res.at[k, rows_of(core * 192, 192)]
        return make(90 + k, ref, ref, pc, h)

    def more_copy(k, part, i):
        src = stage.at[k % 4, :, place(part, 0), columns[part]]
        dst = from_more.at[k, i, :, :, columns[part]]
        return make(106 + len(more) * (2 * k + part + 1) + i, src, dst, more[i], h)

    def out_copy(k):
        return local(8 + k, res.at[k], res_h.at[k])

    def add(k, part, level, other):
        start, count = place_start(part, level), (48, 96, 192)[level]
        cols = slice(0, D) if level == 2 else slice(384 * part, 384 * part + 384)

        @pl.loop(0, count // 48 * 4)
        def _(i):
            z, block = i % 4, i // 4
            mine = rows_of(start + 48 * block, 48)
            theirs = rows_of(48 * block, 48)
            total = stage[k % 4, z, mine, cols].astype(F32) + other[z, theirs, cols].astype(F32)
            stage[k % 4, z, mine, cols] = total.astype(BF)

    def stage_core(k):
        core_copy(k).wait()
        add(k, 0, 2, from_core.at[k])
        for part in range(2):
            a_copy(k, part).start()

    def stage_a(k):
        for part in range(2):
            a_copy(k, part).wait()
            add(k, part, 1, from_a.at[k])
            b_copy(k, part).start()

    def stage_b(k):
        for part in range(2):
            b_copy(k, part).wait()
            add(k, part, 0, from_b.at[k])
            for i in range(len(more)):
                more_copy(k, part, i).start()
                more_copy(k, part, i).wait()
                get = local(8 + k, from_more.at[k, i], from_b.at[k])
                get.start()
                get.wait()
                add(k, part, 0, from_b.at[k])
            for d in (2, 1, 3):
                z_copy(k, part, d).start()

    def stage_z(k):
        for part in range(2):
            cols = slice(384 * part, 384 * part + 384)
            total = stage[k % 4, h, place(part, 0), cols].astype(F32)
            for d in (1, 2, 3):
                z_copy(k, part, d).wait()
                total += from_z[k, d - 1, :, cols].astype(F32)
            res[k, place(part, 0), cols] = total.astype(BF)
            gather_copy(k, part, 0).start()

    def stage_y(k):
        for part in range(2):
            gather_copy(k, part, 0).wait()
            gather_copy(k, part, 1).start()

    def stage_x(k):
        for part in range(2):
            gather_copy(k, part, 1).wait()
        last_copy(k).start()

    def stage_out(k):
        last_copy(k).wait()
        out_copy(k).start()

    vec_steps = [(pc, h), (px, h), (py, h)] + [(m, h) for m in more] + [(b, hp), (b, hq)]

    def vec_copy(i):
        return make(101 + i, vec, vec_in.at[i], *vec_steps[i])

    def stage_vec(i):
        vec_copy(i).wait()
        vec[...] += vec_in[i]
        if i + 1 < len(vec_steps):
            vec_copy(i + 1).start()

    stages = {
        "c": stage_core, "a": stage_a, "b": stage_b, "z": stage_z, "y": stage_y, "x": stage_x, "o": stage_out,
        "v": stage_vec,
    }

    def run(*items):
        for kind, k in items:
            stages[kind](k)

    def reduce_chunk(k, half):
        for z in range(4):
            grad = dot_tn(wide_a[z, :, 384 * half : 384 * half + 384], four[1])
            stage[k, z] = grad.astype(BF)

    def expand_chunk(k, half):
        for z in range(4):
            grad = dot_tn(four[0, :, 384 * half : 384 * half + 384], wide_b[z])
            stage[k, z] = grad.astype(BF)

    def weight_grad(k, start, product):
        for half in range(2):
            grad = product(slice(384 * half, 384 * half + 384)).astype(BF)
            for z in range(2):
                stage[k, 2 * half + z, start : start + SLOT, :] = grad[SLOT * z : SLOT * z + SLOT, :]

    def to_keys(source, target):
        @pl.loop(0, 32)
        def _(i):
            rows = pl.ds(pl.multiple_of(i * 16, 16), 16)
            parts = [source[t, rows, :].astype(F32) for t in range(3)]
            for kb in range(4):
                total = parts[0] * masks[0, kb : kb + 1, :]
                for t in (1, 2):
                    total += parts[t] * masks[t, kb : kb + 1, :]
                target[kb, rows, :] = total.astype(BF)

    def fetch(i, slot):
        g, t = i // 3, i % 3
        tile = (pl.ds(pl.multiple_of(t * TILE, TILE), TILE), pl.ds(pl.multiple_of(g * 256, 256), 256))
        pairs = (
            (p_h.at[i], p_v), (ks_h.at[i], ks_v), (vs_h.at[i], vs_v),
            (q_h.at[tile], q_v), (delta_h.at[tile], d_v), (att_h.at[tile], a_v),
        )
        return [pltpu.make_async_copy(src, dst.at[slot], flow.at[n, slot]) for n, (src, dst) in enumerate(pairs)]

    loads[0].wait()
    loads[1].wait()
    for c in loads[2:] + fetch(0, 0):
        c.start()
    reduce_chunk(0, 0)
    pl.semaphore_wait(barrier, len(targets))
    core_copy(0).start()
    reduce_chunk(1, 1)
    core_copy(1).start()
    run(("c", 0))
    loads[2].wait()
    loads[3].wait()
    expand_chunk(2, 0)
    core_copy(2).start()
    run(("c", 1))
    expand_chunk(3, 1)
    core_copy(3).start()

    left = left_lanes(TILE)
    plan = {
        0: (("c", 2),),
        1: (("a", 0),),
        3: (("a", 1),),
        4: (("c", 3),),
        5: (("a", 2),),
        6: (("b", 0),),
        7: (("b", 1),),
        8: (("a", 3),),
    }

    @pl.loop(0, 9)
    def _(i):
        slot = i % 2
        g, t = i // 3, i % 3
        lanes = pl.multiple_of(g * 256, 256)

        @pl.when(i < 8)
        def _():
            for c in fetch(i + 1, 1 - slot):
                c.start()

        for c in fetch(i, slot):
            c.wait()
        for pair in range(2):
            at = slice(128 * pair, 128 * pair + 128)
            q = q_v[slot, :, at]
            delta = d_v[slot, :, at]
            keys = ks_v[slot, :, at]
            values = vs_v[slot, :, at]
            prod = delta.astype(F32) * a_v[slot, :, at].astype(F32)
            dq, dk, dv = [], [], []
            for side in range(2):
                mask = left if side == 0 else jnp.logical_not(left)
                inner = jnp.sum(jnp.where(mask, prod, 0.0), axis=-1, keepdims=True)
                delta_side = jnp.where(mask, delta, jnp.zeros_like(delta))
                probs = p_v[slot, 2 * pair + side]
                dp = dot_nt(delta_side, values)
                ds = (probs.astype(F32) * (dp - inner)).astype(BF)
                dv.append(dot_tn(probs, delta_side))
                dk.append(dot_tn(ds, jnp.where(mask, q, jnp.zeros_like(q))))
                dq.append(dot_nn(ds, keys))
            where = pl.ds(pl.multiple_of(lanes + 128 * pair, 128), 128)
            wide_a[t, 0:BLOCK, where] = ((dk[0] + dk[1]) * SCALE).astype(BF)
            wide_b[t, 0:BLOCK, where] = (dv[0] + dv[1]).astype(BF)
            wide_a[3, pl.ds(pl.multiple_of(t * TILE, TILE), TILE), where] = (
                jnp.where(left, dq[0], dq[1]) * SCALE
            ).astype(BF)
        for n, items in plan.items():

            @pl.when(i == n)
            def _():
                run(*items)

    run(("z", 0))
    loads[4].wait()
    loads[5].wait()
    weight_grad(0, 0, lambda at: dot_tn(four[2, :, at], four[3]))
    to_keys(wide_b, dv_low)
    get_x = [local(16 + kb, xw_h.at[pl.ds(BLOCK * kb, BLOCK)], wide_b.at[kb, pl.ds(0, BLOCK)]) for kb in range(4)]
    for c in get_x:
        c.start()
    run(("b", 2))
    own_at = own_offset(h)
    own_x = [
        local(32 + c, xw_h.at[pl.ds(pl.multiple_of(own_at + TILE * c, TILE), TILE)], own_v.at[pl.ds(TILE * c, TILE)])
        for c in range(3)
    ]
    for c in own_x:
        c.start()
    to_keys(wide_a, four)
    get_w = [
        local(20 + 4 * m + s, wt_h.at[s, m], wide_a.at[m, pl.ds(SLOT * s, SLOT)]) for m in range(3) for s in range(4)
    ]
    for c in get_w:
        c.start()
    for c in get_x:
        c.wait()

    def x_rows():
        return wide_b[:, 0:BLOCK, :].reshape(WINDOW, D)

    weight_grad(0, SLOT, lambda at: dot_tn(dv_low[:, :, at].reshape(WINDOW, 384), x_rows()))
    core_copy(4).start()
    run(("z", 1), ("b", 3))
    vec[...] = sums_in[...]
    vec[10:11, :] = column_sum(wide_a[3].astype(F32))
    vec[11:12, :] = (
        column_sum(dv_low[0].astype(F32))
        + column_sum(dv_low[1].astype(F32))
        + column_sum(dv_low[2].astype(F32))
        + column_sum(dv_low[3].astype(F32))
    )
    vec_copy(0).start()
    run(("c", 4), ("y", 0))
    for c in get_w:
        c.wait()
    loads[6].wait()
    pair_at = own_offset(hp)
    mid_at = pl.multiple_of(1536 * (h % 2), 256)

    def row_part(start):
        kb, rows = start // BLOCK, pl.ds(pl.multiple_of(start % BLOCK, TILE), TILE)
        return dot_nn(four[kb, rows, :], wide_a[1]) + dot_nn(dv_low[kb, rows, :], wide_a[2])

    def pair_copy(c):
        part = pl.ds(TILE * c, TILE)
        return make(96 + c, dx_v.at[part], dx_pair.at[part], b, hp)

    def mid_copy(c):
        part = pl.ds(TILE * c, TILE)
        return make(99 + c, mid_v.at[part], dx_mid.at[part], b, hm)

    def pair_part(c):
        dx_v[TILE * c : TILE * c + TILE, :] = row_part(pair_at + TILE * c).astype(BF)

    def mid_part(c):
        @pl.when(middle)
        def _():
            mid_v[TILE * c : TILE * c + TILE, :] = row_part(mid_at + TILE * c).astype(BF)

    def mid_start(c):
        @pl.when(middle)
        def _():
            mid_copy(c).start()

    def own_part(c):
        rows = slice(TILE * c, TILE * c + TILE)
        own[rows, :] += row_part(own_at + TILE * c) + dot_nn(wide_a[3, rows, :], wide_a[0])

    pair_part(0)
    pair_copy(0).start()
    pair_part(1)
    pair_copy(1).start()
    run(("y", 1), ("v", 0), ("z", 2))
    mid_part(0)
    mid_start(0)
    weight_grad(1, 0, lambda at: dot_tn(four[:, 0:BLOCK, at].reshape(WINDOW, 384), x_rows()))
    run(("x", 0), ("v", 1))
    for c in own_x:
        c.wait()
    weight_grad(1, SLOT, lambda at: dot_tn(wide_a[3, :, at], own_v[...]))
    core_copy(5).start()
    run(("a", 4), ("z", 3), ("y", 2))
    pair_part(2)
    run(("c", 5), ("x", 1), ("v", 2))
    mid_part(1)
    own_part(0)
    run(("b", 4), ("y", 3), ("x", 2))
    own_part(1)
    run(("v", 3),)
    own_part(2)
    run(("o", 0), ("o", 1), ("a", 5), ("x", 3), ("v", 4), ("b", 5))
    pair_copy(2).start()
    mid_start(1)
    run(("o", 2), ("z", 4), ("o", 3), ("y", 4), ("x", 4), ("z", 5), ("o", 4), ("y", 5))
    for i in range(5, len(vec_steps)):
        run(("v", i))
    sums_o[...] = vec[...]
    run(("x", 5),)
    for c in range(3):
        pair_copy(c).wait()
        rows = slice(TILE * c, TILE * c + TILE)
        own[rows, :] += dx_pair[rows, :].astype(F32)

    @pl.when(middle)
    def _():
        for c in range(2):
            mid_copy(c).wait()
            rows = pl.ds(pl.multiple_of(256 * (h % 2) + TILE * c, TILE), TILE)
            own[rows, :] += dx_mid[TILE * c : TILE * c + TILE, :].astype(F32)

    tg_o[...] = own[...].astype(BF)
    run(("o", 5),)
    for k in range(CHUNKS):
        out_copy(k).wait()


def finish(nb, *args):
    hb = pl.BlockSpec(memory_space=pl.ANY)
    vm = pl.BlockSpec(memory_space=pltpu.VMEM)
    extra = max(0, nb.bit_length() - 4)
    count = 106 + extra * (2 * CHUNKS + 1)
    return pl.pallas_call(
        functools.partial(finish_kernel, nb),
        out_shape=(
            jax.ShapeDtypeStruct((CHUNKS, 384, D), BF),
            jax.ShapeDtypeStruct((ROWS, D), BF),
            jax.ShapeDtypeStruct((16, D), F32),
            jax.ShapeDtypeStruct((CHUNKS, extra, 4, 48, D) if extra else (1, 1, 1, 16, 128), BF),
        ),
        in_specs=[hb] * 14 + [vm] * 2,
        out_specs=(hb, vm, vm, hb),
        scratch_shapes=[
            pltpu.VMEM((4, 4, 384, D), BF),
            pltpu.VMEM((CHUNKS, 4, 192, D), BF),
            pltpu.VMEM((CHUNKS, 4, 96, D), BF),
            pltpu.VMEM((CHUNKS, 4, 48, D), BF),
            pltpu.VMEM((CHUNKS, 3, 48, D), BF),
            pltpu.VMEM((CHUNKS, 384, D), BF),
            pltpu.VMEM((ROWS, D), BF),
            pltpu.VMEM((BLOCK, D), BF),
            pltpu.VMEM((16, D), F32),
            pltpu.VMEM((5 + extra, 16, D), F32),
            pltpu.VMEM((4, ROWS, D), BF),
            pltpu.VMEM((4, ROWS, D), BF),
            pltpu.VMEM((4, ROWS, D), BF),
            pltpu.VMEM((4, BLOCK, D), BF),
            pltpu.VMEM((ROWS, D), F32),
            pltpu.VMEM((2, 4, TILE, BLOCK), BF),
            pltpu.VMEM((2, BLOCK, 256), BF),
            pltpu.VMEM((2, BLOCK, 256), BF),
            pltpu.VMEM((2, TILE, 256), BF),
            pltpu.VMEM((2, TILE, 256), BF),
            pltpu.VMEM((2, TILE, 256), BF),
            pltpu.VMEM((ROWS, D), BF),
            pltpu.VMEM((BLOCK, D), BF),
            pltpu.VMEM((ROWS, D), BF),
            pltpu.SemaphoreType.DMA((35,)),
            pltpu.SemaphoreType.DMA((6, 2)),
            pltpu.SemaphoreType.DMA((count,)),
            pltpu.SemaphoreType.DMA((count,)),
        ],
        compiler_params=pltpu.CompilerParams(
            collective_id=1, has_side_effects=True, vmem_limit_bytes=63 * 2**20
        ),
        name="finish",
    )(*args)


def layer(
    nb, tokens, query_weight, key_weight, value_weight, query_bias, value_bias, mixer_weight, mixer_bias,
    first_gain, first_shift, expand_weight, expand_bias, reduce_weight, reduce_bias, second_gain,
    second_shift, cotangent, group_kinds, pair_orders, triple_orders,
):
    h = lax.axis_index("head")
    xw, wt, qbs, vbs, pairs, triples = start_exchange(
        tokens,
        query_weight.T,
        key_weight.T,
        value_weight.T,
        query_bias.reshape(1, -1),
        value_bias.reshape(1, -1),
        pair_orders.transpose(0, 2, 1),
        triple_orders.transpose(1, 0, 2),
    )
    probs, att, inv, q, keys, values, masks = attend(group_kinds, pairs, triples, qbs, vbs, xw, wt)
    vecs = [
        v.reshape(1, -1)
        for v in (mixer_bias, first_gain, first_shift, reduce_bias, second_gain, second_shift, expand_bias)
    ]
    layer_output, mixed_delta, delta, low, rdel, mdel, act, hdel, sums = dense(
        att, tokens, cotangent, mixer_weight, expand_weight, reduce_weight, inv, *vecs
    )
    res, tokens_grad, sums, _ = finish(
        nb, act, hdel, low, rdel, att, mdel, probs, keys, values, q, delta, xw, wt, mixed_delta, masks, sums
    )
    expand_grad = res[2:4].reshape(D, D).astype(F32)
    reduce_grad = res[0:2].reshape(D, D).astype(F32)
    mixer_grad = res[4, 0:SLOT].astype(F32)
    value_grad = res[4, SLOT:].astype(F32).T
    key_grad = res[5, 0:SLOT].astype(F32).T
    query_grad = res[5, SLOT:].astype(F32).T
    biases = lax.dynamic_slice(sums, (10, SLOT * h), (2, SLOT))
    return (
        layer_output,
        tokens_grad,
        query_grad,
        key_grad,
        value_grad,
        biases[0],
        biases[1],
        mixer_grad,
        sums[0],
        sums[1],
        sums[2],
        expand_grad,
        sums[6:10].reshape(FF),
        reduce_grad,
        sums[3],
        sums[4],
        sums[5],
    )


def solution(mesh):
    rows = P(("batch", "head"), None)
    return jax.shard_map(
        functools.partial(layer, mesh.shape["batch"]),
        mesh=mesh,
        in_specs=(
            rows,
            P(None, "head"),
            P(None, "head"),
            P(None, "head"),
            P("head"),
            P("head"),
            P(),
            P(),
            P(),
            P(),
            P(),
            P(),
            P(),
            P(),
            P(),
            P(),
            rows,
            P("batch"),
            P("batch", "head", None),
            P("batch", "head", None),
        ),
        out_specs=(
            rows,
            rows,
            P(None, "head"),
            P(None, "head"),
            P(None, "head"),
            P("head"),
            P("head"),
            P("head", None),
            P(),
            P(),
            P(),
            P(None, "head"),
            P(),
            P("head", None),
            P(),
            P(),
            P(),
        ),
        check_vma=False,
    )
```

time: 666 us -> 229 us (0.34); the launches traced: 655 us -> 229 us
  Pallas kernels: 0 us -> 213 us
  waiting for transfers between devices: 187 us -> 0 us
  matrix products: 178 us -> 0 us
  blocking collectives: 163 us -> 0 us
  local copies, waits for them, and re-layouts: 65.3 us -> 9.15 us
  other arithmetic: 35.8 us -> 5.51 us
  between operations: 15.7 us -> 1.42 us
  starting transfers between devices: 9.1 us -> 0 us
    pallas_call x0 -> x4, Pallas kernels: none -> 213 us  [the longest x1 108 us: finish(): pl.pallas_call(functools.partial(finish_kernel, nb), out_shape=(jax.Shape...]
    dot_general x60 -> x0, matrix products: 178 us -> none  [the longest x6 48.5 us: product(): return jnp.dot(matrix_a, matrix_b, preferred_element_type=jnp.float32)]
    psum x2 -> x0, blocking collectives: 163 us -> none  [the longest x1 118 us: per_device(): lax.psum((query_weight_grad, key_weight_grad, value_weight_grad, query_bi...]
    all_gather x1 -> x0, waiting for transfers between devices: 89.5 us -> none  [per_device(): gathered = lax.all_gather(tokens, 'head', axis=0, tiled=True)]
    all_to_all x2 -> x0, waiting for transfers between devices: 66.7 us -> none  [the longest x1 42.6 us: per_device(): lax.all_to_all(attended_back, 'head', split_axis=1, concat_axis=0, tiled=...]
    psum x1 -> x0, waiting for transfers between devices: 30.4 us -> none  [per_device(): lax.psum((query_weight_grad, key_weight_grad, value_weight_grad, query_bi...]
    unnamed x81 -> x17, local copies, waits for them, and re-layouts: 21.6 us -> 1.06 us
    scatter-add x2 -> x0, other arithmetic: 13 us -> none  [the longest x1 6.59 us: per_device(): key_delta = zero_quad.at[chosen, :, head_ids, :].add(key_parts).reshape(a...]
  transfers between devices with their start and end apart: 8 -> 0, of which waited for: 4 -> 0; matrix products, arithmetic and copies ran while one was open for 22% -> 0% of each run, Pallas kernels for 0% -> 0%
where the time goes in v1:
time: 229 us
  Pallas kernels  213 us (93%)
  local copies, waits for them, and re-layouts  9.15 us (4%)
  other arithmetic  5.51 us (2%)
    pallas_call x1, Pallas kernels, finish(): pl.pallas_call(functools.partial(finish_kernel, nb), out_shape=(jax.Shape...  108 us
    pallas_call x1, Pallas kernels, start_exchange(): pl.pallas_call(start_kernel, out_shape=(jax.ShapeDtypeStruct((WINDOW, D),...  40.6 us
    pallas_call x1, Pallas kernels, dense(): pl.pallas_call(dense_kernel, out_shape=(rows, jax.ShapeDtypeStruct((ROWS,...  37 us
    pallas_call x1, Pallas kernels, attend(): pl.pallas_call(attend_kernel, grid=(3, 3), out_shape=(jax.ShapeDtypeStruc...  26.8 us

profile of v1, /device:TPU:0, one launch (start us, length us, event | category | flops | bytes accessed | tf_op | source)
XLA Modules:
  0.0 228.8 jit_solution(7992151540692555424)
XLA Ops:
  1.3 40.6 %start_exchange.1 = (bf16[2048,768]{1,0:T(8,128)(2,1)}, bf16[4,3,192,768]{3,2,1,0:T(8,128)(2,1)}, f32[4,1,192]{2,1,0:T(1,128)}, f32[4,1,192]{2,1,0:T(1,128)}, s3...) custom-call(bf16[768,768]{1,0:T(8,128)(2,1)} %tok_h.1, bf16[192,768]{1,0:T(8,128)(2,1)} %bitcast.34, ...), custom_call_target="tpu_custom_call" | custom-call | tf_op jit(solution)/shard_map/start_exchange/pallas_call | solution.py:181
  41.9 0.0 copy-start.2
  41.9 0.0 copy-start.3
  41.9 0.0 copy-start.4
  41.9 0.0 copy-start.5
  41.9 0.0 copy-start.6
  42.0 0.0 copy-start.7
  42.0 26.8 %attend.1 = (bf16[9,4,256,512]{3,2,1,0:T(8,128)(2,1)}, bf16[768,768]{1,0:T(8,128)(2,1)}, f32[768,768]{1,0:T(8,128)}, bf16[768,768]{1,0:T(8,128)(2,1)}, bf16[9,51...) custom-call(s32[1]{0:T(128)S(6)} %copy.38.kinds, s32[4,3,2,3]{3,2,1,0:T(2,128)} %get-tuple-element.42.pairs, ...), custom_call_target="tpu_custom_call" | custom-call | tf_op jit(solution)/shard_map/attend/pallas_call | solution.py:303
  68.8 0.0 copy-done.2
  68.8 0.6 reshape.80.mb
  69.4 0.0 copy-done.3
  69.4 0.6 reshape.81.g1
  70.0 0.0 copy-done.4
  70.0 0.6 reshape.82.s1
  70.6 0.0 copy-done.5
  70.6 0.6 reshape.83.rb
  71.2 0.0 copy-done.6
  71.2 0.6 reshape.84.g2
  71.7 0.0 copy-done.7
  71.7 0.6 reshape.85.s2
  72.3 37.0 %dense.1 = (bf16[768,768]{1,0:T(8,128)(2,1)}, f32[768,768]{1,0:T(8,128)}, bf16[768,768]{1,0:T(8,128)(2,1)}, bf16[768,768]{1,0:T(8,128)(2,1)}, bf16[768,768]{1,0:...) custom-call(bf16[768,768]{1,0:T(8,128)(2,1)} %get-tuple-element.48.a, ...), custom_call_target="tpu_custom_call" | custom-call | tf_op jit(solution)/shard_map/dense/pallas_call | solution.py:442
  109.3 108.3 %finish.1 = (bf16[6,384,768]{2,1,0:T(8,128)(2,1)}, bf16[768,768]{1,0:T(8,128)(2,1)}, f32[16,768]{1,0:T(8,128)}, bf16[1,1,1,16,128]{4,3,2,1,0:T(8,128)(2,1)}) custom-call(bf16[4,768,768]{2,1,0:T(8,128)(2,1)} %get-tuple-element.51.act_h, bf16[4,768,768]{2,1,0:T(8,128)(2,1)} %get-tuple-element.52.hdel_h, bf16[768,768]{1,0:T(8,128)(2,1)} %get-tuple-element.53.low_h, ...), custom_call_target="tpu_custom_call" | custom-call | tf_op jit(solution)/shard_map/finish/pallas_call | solution.py:887
  217.6 0.0 copy-start
  217.6 2.8 %bitcast_convert_fusion.2 = (f32[192,768]{1,0:T(8,128)}, f32[768,192]{0,1:T(8,128)}, f32[768,192]{0,1:T(8,128)}, f32[768,192]{0,1:T(8,128)}) fusion(bf16[6,384,768]{2,1,0:T(8,128)(2,1)} %get-tuple-element.65), kind=kLoop, calls=%fused_computation.5 | loop fusion | flops 589824 | bytes 3538944 | tf_op jit(solution)/shard_map/convert_element_type | solution.py:963
  220.4 1.4 fusion.1
  221.8 1.6 slice_reduce_fusion
  223.5 0.0 copy-done
  223.5 0.2 fusion
  223.6 0.0 copy-start.1
  223.6 2.7 %bitcast_convert_fusion = (f32[768,768]{1,0:T(8,128)}, f32[768,768]{1,0:T(8,128)}) fusion(bf16[2,384,768]{2,1,0:T(8,128)(2,1)S(1)} %get-tuple-element.73, bf16[2,384,768]{2,1,0:T(8,128)(2,1)S(1)} %get-tuple-element.74), kind=kLoop, calls=%fused_computation | loop fusion | flops 1179648 | bytes 7077888 | tf_op jit(solution)/shard_map/convert_element_type | solution.py:962
  226.3 0.8 slice.55
  227.1 0.6 reshape.87
  227.7 0.0 copy-done.1
  227.7 1.0 copy.39
Async XLA Ops:
  41.9 26.9 %copy-start.2 = (f32[768]{0:T(1024)S(1)}, f32[768]{0:T(1024)}, u32[]{:S(2)}) copy-start(f32[768]{0:T(1024)} %param.27) | copy-start | bytes 9220
  41.9 27.5 %copy-start.3 = (f32[768]{0:T(1024)S(1)}, f32[768]{0:T(1024)}, u32[]{:S(2)}) copy-start(f32[768]{0:T(1024)} %param.28) | copy-start | bytes 9220
  41.9 28.1 %copy-start.4 = (f32[768]{0:T(1024)S(1)}, f32[768]{0:T(1024)}, u32[]{:S(2)}) copy-start(f32[768]{0:T(1024)} %param.29) | copy-start | bytes 9220
  41.9 28.6 %copy-start.5 = (f32[768]{0:T(1024)S(1)}, f32[768]{0:T(1024)}, u32[]{:S(2)}) copy-start(f32[768]{0:T(1024)} %param.33) | copy-start | bytes 9220
  41.9 29.2 %copy-start.6 = (f32[768]{0:T(1024)S(1)}, f32[768]{0:T(1024)}, u32[]{:S(2)}) copy-start(f32[768]{0:T(1024)} %param.34) | copy-start | bytes 9220
  42.0 29.8 %copy-start.7 = (f32[768]{0:T(1024)S(1)}, f32[768]{0:T(1024)}, u32[]{:S(2)}) copy-start(f32[768]{0:T(1024)} %param.35) | copy-start | bytes 9220
  217.6 5.9 %copy-start = (bf16[6,384,768]{2,1,0:T(8,128)(2,1)S(1)}, bf16[6,384,768]{2,1,0:T(8,128)(2,1)}, u32[]{:S(2)}) copy-start(bf16[6,384,768]{2,1,0:T(8,128)(2,1)} %get-tuple-element.65) | copy-start | bytes 10616836
  223.6 4.1 %copy-start.1 = (bf16[768,768]{1,0:T(8,128)(2,1)S(1)}, bf16[768,768]{1,0:T(8,128)(2,1)}, u32[]{:S(2)}) copy-start(bf16[768,768]{1,0:T(8,128)(2,1)} %get-tuple-element.101) | copy-start | bytes 3538948

commit v2 on v1

--- a/solution.py
+++ b/solution.py
@@ -25,6 +25,7 @@
 SCALE = 1.0 / math.sqrt(HEAD_SIZE)
 EXP2_SCALE = SCALE * math.log2(math.e)
 CHUNKS = 6
+PIECES = ((0, 0, 384), (1, 0, 384), (2, 0, 384), (3, 0, 384), (4, 0, 384), (5, 0, 256), (5, 256, 128))
 
 
 def dot_nn(a, b):
@@ -380,32 +381,36 @@
     for c in loads:
         c.start()
     sums_o[...] = jnp.zeros_like(sums_o)
+
+    def row(ref):
+        return ref[...].reshape(1, -1)
+
     for c in loads:
         c.wait()
 
     @pl.loop(0, 3)
     def _(t):
         at = pl.ds(pl.multiple_of(t * TILE, TILE), TILE)
-        mixed = dot_nn(att[at, :], mw[...]) + mb[...] + tok[at, :].astype(F32)
+        mixed = dot_nn(att[at, :], mw[...]) + row(mb) + tok[at, :].astype(F32)
         scaled_one, inverse_one = norm_parts(mixed)
-        normed = scaled_one * g1[...] + s1[...]
+        normed = scaled_one * row(g1) + row(s1)
         normed_low = normed.astype(BF)
         low[at, :] = normed_low
-        branch = rb[...] + normed
+        branch = row(rb) + normed
         for j in range(4):
             cols = slice(768 * j, 768 * j + 768)
-            hidden = dot_nn(normed_low, ew[:, cols]) + eb[:, cols]
+            hidden = dot_nn(normed_low, ew[:, cols]) + row(eb)[:, cols]
             phi_sum, bell = normal_parts(hidden)
             active = (hidden * phi_sum).astype(BF)
             act[j, at, :] = active
             slope[:, cols] = (phi_sum + hidden * bell).astype(BF)
             branch += dot_nn(active, rw[cols, :])
         scaled_two, inverse_two = norm_parts(branch)
-        out_o[at, :] = (scaled_two * g2[...] + s2[...]).astype(BF)
+        out_o[at, :] = (scaled_two * row(g2) + row(s2)).astype(BF)
         upstream = cot[at, :].astype(F32)
         sums_o[4:5, :] += column_sum(upstream * scaled_two)
         sums_o[5:6, :] += column_sum(upstream)
-        branch_delta = norm_back(upstream * g2[...], scaled_two, inverse_two)
+        branch_delta = norm_back(upstream * row(g2), scaled_two, inverse_two)
         reduce_delta = branch_delta.astype(BF)
         rdel[at, :] = reduce_delta
         sums_o[3:4, :] += column_sum(reduce_delta.astype(F32))
@@ -419,7 +424,7 @@
             normed_delta += dot_nt(back_low, ew[:, cols])
         sums_o[1:2, :] += column_sum(normed_delta * scaled_one)
         sums_o[2:3, :] += column_sum(normed_delta)
-        mixed_delta = norm_back(normed_delta * g1[...], scaled_one, inverse_one)
+        mixed_delta = norm_back(normed_delta * row(g1), scaled_one, inverse_one)
         mixed_o[at, :] = mixed_delta
         mixer_delta = mixed_delta.astype(BF)
         mdel[at, :] = mixer_delta
@@ -519,117 +524,134 @@
     def rows_of(start, count):
         return pl.ds(pl.multiple_of(start, 16), count)
 
-    def place_start(part, level):
-        start = core * 192
+    def size(n, level):
+        return (PIECES[n][2] // 8, PIECES[n][2] // 4, PIECES[n][2] // 2)[level]
+
+    def place_start(n, part, level):
+        start = PIECES[n][1] + core * size(n, 2)
         if level < 2:
-            start = start + bits[part][0] * 96
+            start = start + bits[part][0] * size(n, 1)
         if level < 1:
-            start = start + bits[part][2] * 48
+            start = start + bits[part][2] * size(n, 0)
         return start
 
-    def place(part, level):
-        return rows_of(place_start(part, level), (48, 96, 192)[level])
-
-    def core_copy(k):
-        return make(k, stage.at[k % 4, :, rows_of((1 - core) * 192, 192)], from_core.at[k], pc, h)
-
-    def a_copy(k, part):
+    def place(n, part, level):
+        return rows_of(place_start(n, part, level), size(n, level))
+
+    def landing(n, level):
+        return slice(PIECES[n][1] * size(n, level) // PIECES[n][2], (PIECES[n][1] + PIECES[n][2]) * size(n, level) // PIECES[n][2])
+
+    def land(ref, n, level, cols):
+        rows = landing(n, level)
+        return ref.at[PIECES[n][0], :, pl.ds(rows.start, rows.stop - rows.start), cols]
+
+    def core_copy(n):
+        k, first, _ = PIECES[n]
+        src = stage.at[k % 4, :, rows_of(first + (1 - core) * size(n, 2), size(n, 2))]
+        return make(n, src, land(from_core, n, 2, slice(None)), pc, h)
+
+    def a_copy(n, part):
+        k, first, _ = PIECES[n]
         a_bit, who = bits[part][:2]
-        src = stage.at[k % 4, :, rows_of(core * 192 + (1 - a_bit) * 96, 96), columns[part]]
-        return make(6 + 2 * k + part, src, from_a.at[k, :, :, columns[part]], who, h)
-
-    def b_copy(k, part):
-        a_bit, _, b_bit, who = bits[part]
-        src = stage.at[k % 4, :, rows_of(core * 192 + a_bit * 96 + (1 - b_bit) * 48, 48), columns[part]]
-        return make(18 + 2 * k + part, src, from_b.at[k, :, :, columns[part]], who, h)
-
-    def z_copy(k, part, d):
+        rows = rows_of(first + core * size(n, 2) + (1 - a_bit) * size(n, 1), size(n, 1))
+        return make(7 + 2 * n + part, stage.at[k % 4, :, rows, columns[part]], land(from_a, n, 1, columns[part]), who, h)
+
+    def b_copy(n, part):
+        k = PIECES[n][0]
+        _, _, b_bit, who = bits[part]
+        rows = rows_of(place_start(n, part, 1) + (1 - b_bit) * size(n, 0), size(n, 0))
+        return make(21 + 2 * n + part, stage.at[k % 4, :, rows, columns[part]], land(from_b, n, 0, columns[part]), who, h)
+
+    def z_copy(n, part, d):
         o = others[d - 1]
-        src = stage.at[k % 4, o, place(part, 0), columns[part]]
-        return make(30 + 6 * k + 3 * part + d - 1, src, from_z.at[k, d - 1, :, columns[part]], b, o)
-
-    def gather_copy(k, part, level):
-        ref = res.at[k, place(part, level), columns[part]]
-        return make(66 + 12 * level + 2 * k + part, ref, ref, bits[part][3 if level == 0 else 1], h)
-
-    def last_copy(k):
-        ref = res.at[k, rows_of(core * 192, 192)]
-        return make(90 + k, ref, ref, pc, h)
-
-    def more_copy(k, part, i):
-        src = stage.at[k % 4, :, place(part, 0), columns[part]]
-        dst = from_more.at[k, i, :, :, columns[part]]
-        return make(106 + len(more) * (2 * k + part + 1) + i, src, dst, more[i], h)
+        k = PIECES[n][0]
+        rows = landing(n, 0)
+        dst = from_z.at[k, d - 1, pl.ds(rows.start, rows.stop - rows.start), columns[part]]
+        return make(35 + 6 * n + 3 * part + d - 1, stage.at[k % 4, o, place(n, part, 0), columns[part]], dst, b, o)
+
+    def gather_copy(n, part, level):
+        ref = res.at[PIECES[n][0], place(n, part, level), columns[part]]
+        return make(77 + 14 * level + 2 * n + part, ref, ref, bits[part][3 if level == 0 else 1], h)
+
+    def last_copy(n):
+        ref = res.at[PIECES[n][0], place(n, 0, 2)]
+        return make(105 + n, ref, ref, pc, h)
+
+    def more_copy(n, part, i):
+        src = stage.at[PIECES[n][0] % 4, :, place(n, part, 0), columns[part]]
+        dst = from_more.at[n, i, :, pl.ds(0, size(n, 0)), columns[part]]
+        return make(122 + len(more) * (2 * n + part + 1) + i, src, dst, more[i], h)
 
     def out_copy(k):
         return local(8 + k, res.at[k], res_h.at[k])
 
-    def add(k, part, level, other):
-        start, count = place_start(part, level), (48, 96, 192)[level]
+    def add(n, part, level, other):
+        k, block = PIECES[n][0] % 4, size(n, 0)
+        start, first = place_start(n, part, level), landing(n, level).start
         cols = slice(0, D) if level == 2 else slice(384 * part, 384 * part + 384)
 
-        @pl.loop(0, count // 48 * 4)
+        @pl.loop(0, size(n, level) // block * 4)
         def _(i):
-            z, block = i % 4, i // 4
-            mine = rows_of(start + 48 * block, 48)
-            theirs = rows_of(48 * block, 48)
-            total = stage[k % 4, z, mine, cols].astype(F32) + other[z, theirs, cols].astype(F32)
-            stage[k % 4, z, mine, cols] = total.astype(BF)
-
-    def stage_core(k):
-        core_copy(k).wait()
-        add(k, 0, 2, from_core.at[k])
+            z, at = i % 4, i // 4 * block
+            mine = rows_of(start + at, block)
+            stage[k, z, mine, cols] = stage[k, z, mine, cols] + other[PIECES[n][0], z, rows_of(first + at, block), cols]
+
+    def stage_core(n):
+        core_copy(n).wait()
+        add(n, 0, 2, from_core)
         for part in range(2):
-            a_copy(k, part).start()
-
-    def stage_a(k):
+            a_copy(n, part).start()
+
+    def stage_a(n):
         for part in range(2):
-            a_copy(k, part).wait()
-            add(k, part, 1, from_a.at[k])
-            b_copy(k, part).start()
-
-    def stage_b(k):
+            a_copy(n, part).wait()
+            add(n, part, 1, from_a)
+            b_copy(n, part).start()
+
+    def stage_b(n):
         for part in range(2):
-            b_copy(k, part).wait()
-            add(k, part, 0, from_b.at[k])
+            b_copy(n, part).wait()
+            add(n, part, 0, from_b)
             for i in range(len(more)):
-                more_copy(k, part, i).start()
-                more_copy(k, part, i).wait()
-                get = local(8 + k, from_more.at[k, i], from_b.at[k])
+                more_copy(n, part, i).start()
+                more_copy(n, part, i).wait()
+                get = local(7, from_more.at[n, i, :, pl.ds(0, size(n, 0))], land(from_b, n, 0, slice(None)))
                 get.start()
                 get.wait()
-                add(k, part, 0, from_b.at[k])
+                add(n, part, 0, from_b)
             for d in (2, 1, 3):
-                z_copy(k, part, d).start()
-
-    def stage_z(k):
+                z_copy(n, part, d).start()
+
+    def stage_z(n):
+        k, rows = PIECES[n][0], landing(n, 0)
         for part in range(2):
             cols = slice(384 * part, 384 * part + 384)
-            total = stage[k % 4, h, place(part, 0), cols].astype(F32)
+            total = stage[k % 4, h, place(n, part, 0), cols].astype(F32)
             for d in (1, 2, 3):
-                z_copy(k, part, d).wait()
-                total += from_z[k, d - 1, :, cols].astype(F32)
-            res[k, place(part, 0), cols] = total.astype(BF)
-            gather_copy(k, part, 0).start()
-
-    def stage_y(k):
+                z_copy(n, part, d).wait()
+                total += from_z[k, d - 1, rows, cols].astype(F32)
+            res[k, place(n, part, 0), cols] = total.astype(BF)
+            gather_copy(n, part, 0).start()
+
+    def stage_y(n):
         for part in range(2):
-            gather_copy(k, part, 0).wait()
-            gather_copy(k, part, 1).start()
-
-    def stage_x(k):
+            gather_copy(n, part, 0).wait()
+            gather_copy(n, part, 1).start()
+
+    def stage_x(n):
         for part in range(2):
-            gather_copy(k, part, 1).wait()
-        last_copy(k).start()
-
-    def stage_out(k):
-        last_copy(k).wait()
-        out_copy(k).start()
+            gather_copy(n, part, 1).wait()
+        last_copy(n).start()
+
+    def stage_out(n):
+        last_copy(n).wait()
+        if n != len(PIECES) - 2:
+            out_copy(PIECES[n][0]).start()
 
     vec_steps = [(pc, h), (px, h), (py, h)] + [(m, h) for m in more] + [(b, hp), (b, hq)]
 
     def vec_copy(i):
-        return make(101 + i, vec, vec_in.at[i], *vec_steps[i])
+        return make(117 + i, vec, vec_in.at[i], *vec_steps[i])
 
     def stage_vec(i):
         vec_copy(i).wait()
@@ -808,11 +830,11 @@
 
     def pair_copy(c):
         part = pl.ds(TILE * c, TILE)
-        return make(96 + c, dx_v.at[part], dx_pair.at[part], b, hp)
+        return make(112 + c, dx_v.at[part], dx_pair.at[part], b, hp)
 
     def mid_copy(c):
         part = pl.ds(TILE * c, TILE)
-        return make(99 + c, mid_v.at[part], dx_mid.at[part], b, hm)
+        return make(115 + c, mid_v.at[part], dx_mid.at[part], b, hm)
 
     def pair_part(c):
         dx_v[TILE * c : TILE * c + TILE, :] = row_part(pair_at + TILE * c).astype(BF)
@@ -844,23 +866,26 @@
         c.wait()
     weight_grad(1, SLOT, lambda at: dot_tn(wide_a[3, :, at], own_v[...]))
     core_copy(5).start()
+    core_copy(6).start()
     run(("a", 4), ("z", 3), ("y", 2))
     pair_part(2)
-    run(("c", 5), ("x", 1), ("v", 2))
+    run(("c", 5), ("c", 6), ("x", 1), ("v", 2))
     mid_part(1)
     own_part(0)
     run(("b", 4), ("y", 3), ("x", 2))
     own_part(1)
     run(("v", 3),)
     own_part(2)
-    run(("o", 0), ("o", 1), ("a", 5), ("x", 3), ("v", 4), ("b", 5))
+    run(("o", 0), ("o", 1), ("a", 5), ("x", 3), ("v", 4), ("a", 6), ("z", 4), ("b", 5), ("b", 6))
     pair_copy(2).start()
     mid_start(1)
-    run(("o", 2), ("z", 4), ("o", 3), ("y", 4), ("x", 4), ("z", 5), ("o", 4), ("y", 5))
+    run(
+        ("o", 2), ("y", 4), ("o", 3), ("z", 5), ("x", 4), ("y", 5), ("z", 6), ("o", 4), ("x", 5), ("y", 6), ("o", 5),
+        ("x", 6),
+    )
     for i in range(5, len(vec_steps)):
         run(("v", i))
     sums_o[...] = vec[...]
-    run(("x", 5),)
     for c in range(3):
         pair_copy(c).wait()
         rows = slice(TILE * c, TILE * c + TILE)
@@ -874,7 +899,7 @@
             own[rows, :] += dx_mid[TILE * c : TILE * c + TILE, :].astype(F32)
 
     tg_o[...] = own[...].astype(BF)
-    run(("o", 5),)
+    run(("o", 6),)
     for k in range(CHUNKS):
         out_copy(k).wait()
 
@@ -883,14 +908,14 @@
     hb = pl.BlockSpec(memory_space=pl.ANY)
     vm = pl.BlockSpec(memory_space=pltpu.VMEM)
     extra = max(0, nb.bit_length() - 4)
-    count = 106 + extra * (2 * CHUNKS + 1)
+    count = 122 + extra * (2 * len(PIECES) + 1)
     return pl.pallas_call(
         functools.partial(finish_kernel, nb),
         out_shape=(
             jax.ShapeDtypeStruct((CHUNKS, 384, D), BF),
             jax.ShapeDtypeStruct((ROWS, D), BF),
             jax.ShapeDtypeStruct((16, D), F32),
-            jax.ShapeDtypeStruct((CHUNKS, extra, 4, 48, D) if extra else (1, 1, 1, 16, 128), BF),
+            jax.ShapeDtypeStruct((len(PIECES), extra, 4, 48, D) if extra else (1, 1, 1, 16, 128), BF),
         ),
         in_specs=[hb] * 14 + [vm] * 2,
         out_specs=(hb, vm, vm, hb),
@@ -931,12 +956,67 @@
     )(*args)
 
 
+def unpack_kernel(res, sums, reduce_o, expand_o, mixer_o, value_o, key_o, query_o, qbias_o, vbias_o, hidden_o, *vec_o):
+    i = pl.program_id(0)
+    h = lax.axis_index("head")
+
+    @pl.when(i == 0)
+    def _():
+        for n, ref in enumerate(vec_o):
+            ref[...] = sums[n : n + 1, :].reshape(D)
+        for j in range(4):
+            hidden_o[D * j : D * j + D] = sums[6 + j : 7 + j, :].reshape(D)
+        for n, ref in ((10, qbias_o), (11, vbias_o)):
+            mine = sums[n : n + 1, 0:SLOT]
+            for z in range(1, 4):
+                mine = jnp.where(h == z, sums[n : n + 1, SLOT * z : SLOT * z + SLOT], mine)
+            ref[...] = mine.reshape(SLOT)
+
+    @pl.when(i < 2)
+    def _():
+        reduce_o[...] = res[0].astype(F32)
+
+    @pl.when(jnp.logical_and(i >= 2, i < 4))
+    def _():
+        expand_o[...] = res[0].astype(F32)
+
+    @pl.when(i == 4)
+    def _():
+        mixer_o[...] = res[0, 0:SLOT, :].astype(F32)
+        value_o[...] = res[0, SLOT:, :].astype(F32)
+
+    @pl.when(i == 5)
+    def _():
+        key_o[...] = res[0, 0:SLOT, :].astype(F32)
+        query_o[...] = res[0, SLOT:, :].astype(F32)
+
+
+def unpack(res, sums):
+    vm = pl.BlockSpec(memory_space=pltpu.VMEM)
+    square = jax.ShapeDtypeStruct((D, D), F32)
+    strip = jax.ShapeDtypeStruct((SLOT, D), F32)
+    short = jax.ShapeDtypeStruct((SLOT,), F32)
+    row = jax.ShapeDtypeStruct((D,), F32)
+    return pl.pallas_call(
+        unpack_kernel,
+        grid=(CHUNKS,),
+        out_shape=(square, square, strip, strip, strip, strip, short, short, jax.ShapeDtypeStruct((FF,), F32)) + (row,) * 6,
+        in_specs=[pl.BlockSpec((1, 384, D), lambda i: (i, 0, 0)), vm],
+        out_specs=(
+            pl.BlockSpec((384, D), lambda i: (jnp.minimum(i, 1), 0)),
+            pl.BlockSpec((384, D), lambda i: (jnp.clip(i - 2, 0, 1), 0)),
+        )
+        + (vm,) * 13,
+        compiler_params=pltpu.CompilerParams(dimension_semantics=("arbitrary",), vmem_limit_bytes=VMEM_LIMIT),
+        name="unpack",
+    )(res, sums)
+
+
 def layer(
     nb, tokens, query_weight, key_weight, value_weight, query_bias, value_bias, mixer_weight, mixer_bias,
     first_gain, first_shift, expand_weight, expand_bias, reduce_weight, reduce_bias, second_gain,
     second_shift, cotangent, group_kinds, pair_orders, triple_orders,
 ):
-    h = lax.axis_index("head")
     xw, wt, qbs, vbs, pairs, triples = start_exchange(
         tokens,
         query_weight.T,
@@ -948,41 +1028,34 @@
         triple_orders.transpose(1, 0, 2),
     )
     probs, att, inv, q, keys, values, masks = attend(group_kinds, pairs, triples, qbs, vbs, xw, wt)
-    vecs = [
-        v.reshape(1, -1)
-        for v in (mixer_bias, first_gain, first_shift, reduce_bias, second_gain, second_shift, expand_bias)
-    ]
+    vecs = (mixer_bias, first_gain, first_shift, reduce_bias, second_gain, second_shift, expand_bias)
     layer_output, mixed_delta, delta, low, rdel, mdel, act, hdel, sums = dense(
         att, tokens, cotangent, mixer_weight, expand_weight, reduce_weight, inv, *vecs
     )
     res, tokens_grad, sums, _ = finish(
         nb, act, hdel, low, rdel, att, mdel, probs, keys, values, q, delta, xw, wt, mixed_delta, masks, sums
     )
-    expand_grad = res[2:4].reshape(D, D).astype(F32)
-    reduce_grad = res[0:2].reshape(D, D).astype(F32)
-    mixer_grad = res[4, 0:SLOT].astype(F32)
-    value_grad = res[4, SLOT:].astype(F32).T
-    key_grad = res[5, 0:SLOT].astype(F32).T
-    query_grad = res[5, SLOT:].astype(F32).T
-    biases = lax.dynamic_slice(sums, (10, SLOT * h), (2, SLOT))
+    out = unpack(res, sums)
+    reduce_grad, expand_grad, mixer_grad, value_grad, key_grad, query_grad, query_sum, value_sum, hidden_sum = out[:9]
+    mixer_sum, gain_one, shift_one, reduce_sum, gain_two, shift_two = out[9:]
     return (
         layer_output,
         tokens_grad,
-        query_grad,
-        key_grad,
-        value_grad,
-        biases[0],
-        biases[1],
+        query_grad.T,
+        key_grad.T,
+        value_grad.T,
+        query_sum,
+        value_sum,
         mixer_grad,
-        sums[0],
-        sums[1],
-        sums[2],
+        mixer_sum,
+        gain_one,
+        shift_one,
         expand_grad,
-        sums[6:10].reshape(FF),
+        hidden_sum,
         reduce_grad,
-        sums[3],
-        sums[4],
-        sums[5],
+        reduce_sum,
+        gain_two,
+        shift_two,
     )
 
 

time: 229 us -> 224 us (0.978)
  local copies, waits for them, and re-layouts: 9.15 us -> 1.02 us
  Pallas kernels: 213 us -> 221 us
  other arithmetic: 5.51 us -> 0 us
    pallas_call x0 -> x1, Pallas kernels: none -> 7.64 us  [unpack(): pl.pallas_call(unpack_kernel, grid=(CHUNKS,), out_shape=(square, square,...]
    convert_element_type x2 -> x0, other arithmetic: 5.51 us -> none  [the longest x1 2.82 us: layer(): mixer_grad = res[4, 0:SLOT].astype(F32)]
    reshape x7 -> x0, local copies, waits for them, and re-layouts: 4.09 us -> none  [the longest x6 3.48 us: layer(): v.reshape(1, -1)]
    slice x4 -> x0, local copies, waits for them, and re-layouts: 3.99 us -> none  [the longest x1 1.62 us: layer(): sums[5]]
where the time goes in v2:
time: 224 us; the launch traced here: 223 us
  Pallas kernels  221 us (99%)
    pallas_call x1, Pallas kernels, finish(): pl.pallas_call(functools.partial(finish_kernel, nb), out_shape=(jax.Shape...  109 us
    pallas_call x1, Pallas kernels, start_exchange(): pl.pallas_call(start_kernel, out_shape=(jax.ShapeDtypeStruct((WINDOW, D),...  40.6 us
    pallas_call x1, Pallas kernels, dense(): pl.pallas_call(dense_kernel, out_shape=(rows, jax.ShapeDtypeStruct((ROWS,...  37 us
    pallas_call x1, Pallas kernels, attend(): pl.pallas_call(attend_kernel, grid=(3, 3), out_shape=(jax.ShapeDtypeStruc...  26.8 us
    pallas_call x1, Pallas kernels, unpack(): pl.pallas_call(unpack_kernel, grid=(CHUNKS,), out_shape=(square, square,...  7.64 us

profile of v2, /device:TPU:0, one launch (start us, length us, event | category | flops | bytes accessed | tf_op | source)
XLA Modules:
  0.0 223.3 jit_solution(12762186176242295732)
XLA Ops:
  1.3 40.6 %start_exchange.1 = (bf16[2048,768]{1,0:T(8,128)(2,1)}, bf16[4,3,192,768]{3,2,1,0:T(8,128)(2,1)}, f32[4,1,192]{2,1,0:T(1,128)}, f32[4,1,192]{2,1,0:T(1,128)}, s3...) custom-call(bf16[768,768]{1,0:T(8,128)(2,1)} %tok_h.1, bf16[192,768]{1,0:T(8,128)(2,1)} %bitcast.10, ...), custom_call_target="tpu_custom_call" | custom-call | tf_op jit(solution)/shard_map/start_exchange/pallas_call | solution.py:182
  41.9 26.8 %attend.1 = (bf16[9,4,256,512]{3,2,1,0:T(8,128)(2,1)}, bf16[768,768]{1,0:T(8,128)(2,1)}, f32[768,768]{1,0:T(8,128)}, bf16[768,768]{1,0:T(8,128)(2,1)}, bf16[9,51...) custom-call(s32[1]{0:T(128)S(6)} %copy.38.kinds, s32[4,3,2,3]{3,2,1,0:T(2,128)} %get-tuple-element.57.pairs, ...), custom_call_target="tpu_custom_call" | custom-call | tf_op jit(solution)/shard_map/attend/pallas_call | solution.py:304
  68.7 37.0 %dense.1 = (bf16[768,768]{1,0:T(8,128)(2,1)}, f32[768,768]{1,0:T(8,128)}, bf16[768,768]{1,0:T(8,128)(2,1)}, bf16[768,768]{1,0:T(8,128)(2,1)}, bf16[768,768]{1,0:...) custom-call(bf16[768,768]{1,0:T(8,128)(2,1)} %get-tuple-element.63.a, ...), custom_call_target="tpu_custom_call" | custom-call | tf_op jit(solution)/shard_map/dense/pallas_call | solution.py:447
  105.7 108.9 %finish.1 = (bf16[6,384,768]{2,1,0:T(8,128)(2,1)}, bf16[768,768]{1,0:T(8,128)(2,1)}, f32[16,768]{1,0:T(8,128)}, bf16[1,1,1,16,128]{4,3,2,1,0:T(8,128)(2,1)}) custom-call(bf16[4,768,768]{2,1,0:T(8,128)(2,1)} %get-tuple-element.66.act_h, bf16[4,768,768]{2,1,0:T(8,128)(2,1)} %get-tuple-element.67.hdel_h, bf16[768,768]{1,0:T(8,128)(2,1)} %get-tuple-element.68.low_h, ...), custom_call_target="tpu_custom_call" | custom-call | tf_op jit(solution)/shard_map/finish/pallas_call | solution.py:912
  214.6 0.0 copy-start
  214.6 7.6 %unpack.1 = (f32[768,768]{1,0:T(8,128)}, f32[768,768]{1,0:T(8,128)}, f32[192,768]{1,0:T(8,128)}, f32[192,768]{1,0:T(8,128)}, f32[192,768]{1,0:T(8,128)}, /*index...) custom-call(bf16[6,384,768]{2,1,0:T(8,128)(2,1)} %get-tuple-element., ...), custom_call_target="tpu_custom_call" | custom-call | tf_op jit(solution)/shard_map/unpack/pallas_call | solution.py:1000
  222.3 0.0 copy-done
  222.3 1.0 copy.39
Async XLA Ops:
  214.6 7.7 %copy-start = (bf16[768,768]{1,0:T(8,128)(2,1)S(1)}, bf16[768,768]{1,0:T(8,128)(2,1)}, u32[]{:S(2)}) copy-start(bf16[768,768]{1,0:T(8,128)(2,1)} %get-tuple-element.115) | copy-start | bytes 3538948
